TPU v7x, 32 devices: a whole 2x2x4 slice. The times are simulated.
32 devices in a mesh: sea: 2 (over y), tm: 16 (over z, x, core).
Axes of the slice: x: 2, y: 2, z: 4, core: 2. Of those that a mesh axis runs over, the one named last changes fastest.
Arguments:
- wet_station: int32 [16384, 128], P(('sea', 'tm')), parts along dimension 0, may hold values from 0 to 99
- wet_girth: int32 [16384, 128], P(('sea', 'tm')), parts along dimension 0, may hold values from 0 to 499
- wet_count: int32 [16384], P(('sea', 'tm')), parts along dimension 0, may hold values from 1 to 128, as said below
- pressure: bfloat16 [16384, 128], P(('sea', 'tm')), parts along dimension 0, may hold values from -6 to 6
- panel_area: float32 [50000], replicated, may hold values from 0.2 to 2
- panel_patch: int32 [50000], replicated, may hold values from 0 to 3071
- patch_modes: bfloat16 [3072, 64], replicated, may hold values from -0.75 to 0.75
- impulse: bfloat16 [512, 64, 64], replicated, may hold values from -0.03125 to 0.03125
- stress_map: bfloat16 [64, 128], P(None, 'tm'), may hold values from -0.75 to 0.75
Outputs:
- stress: bfloat16 [128, 16384], P('tm', 'sea'), parts along dimension 1
There are 2 independent parts, one for each index of `sea`. A program takes and returns all parts, laid end to end along the dimension named above; an argument that names none is the same for every part. Nothing has to cross between parts.
Inputs may be any that keep to these rules, and one draw needn't show every extreme that they name: `wet_count`: every time step has at least one live slot, and some time step of every draw lists 128 live slots.
All inputs are finite; a program needn't handle non-finite values.
Results may differ from a plain program's by a relative error of at most 0.0058.
Values may be sent and summed in bfloat16 or wider, within the bound.
No kernel may reach another device: no remote copies, remote signals or barrier semaphores. Data moves between devices by JAX's collectives and lax.ppermute only.
A program may use at most 64 MiB of HBM per device.

v0:
```python
import jax
import jax.numpy as jnp
from jax import lax
from jax.sharding import PartitionSpec as P

GIRTH = 500


def shifted(value, axis, steps):
    count = lax.axis_size(axis)
    leading, last = (max(0, -steps), min(count, count - steps))
    return lax.ppermute(value, axis, [(source, source + steps) for source in range(leading, last)])


def block_forcing(block, panel_area, panel_patch, patch_modes):
    stations, girths, counts, press = block
    slots = stations.shape[1]
    panels = stations * GIRTH + girths
    area = panel_area[panels]
    patch = panel_patch[panels]
    live = jnp.arange(slots, dtype=jnp.int32)[None, :] < counts[:, None]
    force = jnp.where(live, press.astype(jnp.float32) * area, jnp.float32(0.0))
    mode_rows = patch_modes[patch].astype(jnp.float32)
    return jnp.einsum("tk,tkm->tm", force, mode_rows, precision=lax.Precision.HIGHEST)


def body(
    wet_station,
    wet_girth,
    wet_count,
    pressure,
    panel_area,
    panel_patch,
    patch_modes,
    impulse,
    stress_map,
):
    steps, slots = wet_station.shape
    lags = impulse.shape[0]
    modes = patch_modes.shape[1]
    rows_block = min(64, steps)
    count_blocks = steps // rows_block
    blocks = (
        wet_station.reshape(count_blocks, rows_block, slots),
        wet_girth.reshape(count_blocks, rows_block, slots),
        wet_count.reshape(count_blocks, rows_block),
        pressure.reshape(count_blocks, rows_block, slots),
    )
    forcing = lax.map(lambda b: block_forcing(b, panel_area, panel_patch, patch_modes), blocks)
    forcing = forcing.reshape(steps, modes).astype(jnp.bfloat16)
    earlier = shifted(forcing[steps - (lags - 1) :], "tm", 1)
    extended = jnp.concatenate([earlier, forcing], 0)
    response = lax.conv_general_dilated(
        extended[None],
        impulse[::-1],
        (1,),
        "VALID",
        dimension_numbers=("NWC", "WIO", "NWC"),
        preferred_element_type=jnp.float32,
    )[0]
    response = response.astype(jnp.bfloat16)
    product = lax.dot_general(
        stress_map,
        lax.all_gather(response, "tm", axis=0, tiled=True),
        (((0,), (1,)), ((), ())),
        preferred_element_type=jnp.float32,
    )
    return product.astype(jnp.bfloat16)


def solution(mesh):
    return jax.shard_map(
        body,
        mesh=mesh,
        in_specs=(
            P(("sea", "tm"), None),
            P(("sea", "tm"), None),
            P(("sea", "tm")),
            P(("sea", "tm"), None),
            P(),
            P(),
            P(),
            P(),
            P(None, "tm"),
        ),
        out_specs=P("tm", "sea"),
        check_vma=False,
    )
```

profile of v0, /device:TPU:0, one launch (start us, length us, event | category | flops | bytes accessed | tf_op | source)
XLA Modules:
  0.0 990.0 jit_solution(16961669696455892847)
XLA Ops:
  7.3 1.4 copy.17
  8.7 884.5 %while.10 = (s32[]{:T(128)}, bf16[8,64,64]{2,1,0:T(8,128)(2,1)S(1)}, s32[8,64]{1,0:T(8,128)S(1)}, bf16[8,64,128]{2,1,0:T(8,128)(2,1)}, s32[8,64,128]{2,1,0:T(8,1...) while((s32[]{:T(128)}, ...), condition=%wide.region_1.2_spmd, body=%wide.region_0.1_spmd.sunk | while | flops 6406146 | bytes 4536473 | solution.py:49
  8.7 0.8 fusion.23
  9.5 37.6 %gather_fusion.1 = s32[8192]{0:T(1024)S(1)} fusion(s32[50000]{0:T(1024)} %get-tuple-element.180, s32[8192]{0:T(1024)S(1)} %fusion.23), kind=kCustom, calls=%fused_computation.1.clone.1 | custom fusion | bytes 98304 | tf_op jit(solution)/shard_map/while/body/eval_jaxpr/gather | solution.py:20
  47.1 45.5 %gather_fusion = f32[8192]{0:T(1024)S(1)} fusion(f32[50000]{0:T(1024)S(1)} %copy-done.1, s32[8192]{0:T(1024)S(1)} %fusion.23), kind=kCustom, calls=%fused_computation.clone.1 | custom fusion | bytes 98304 | tf_op jit(solution)/shard_map/while/body/eval_jaxpr/gather | solution.py:19
  92.7 0.8 fusion.25
  93.5 24.0 %gather_fusion.2 = bf16[8192,64]{1,0:T(8,128)(2,1)S(1)} fusion(bf16[3072,64]{1,0:T(8,128)(2,1)S(1)} %get-tuple-element.181, s32[8192]{0:T(1024)S(1)} %fusion.26), kind=kCustom, calls=%fused_computation.2.clone.1 | custom fusion | bytes 2129920 | tf_op jit(solution)/shard_map/while/body/eval_jaxpr/gather | solution.py:23
  117.5 1.7 fusion.27
  120.1 37.6 %gather_fusion.1 = s32[8192]{0:T(1024)S(1)} fusion(s32[50000]{0:T(1024)} %get-tuple-element.180, s32[8192]{0:T(1024)S(1)} %fusion.23), kind=kCustom, calls=%fused_computation.1.clone.1 | custom fusion | bytes 98304 | tf_op jit(solution)/shard_map/while/body/eval_jaxpr/gather | solution.py:20
  157.7 45.5 %gather_fusion = f32[8192]{0:T(1024)S(1)} fusion(f32[50000]{0:T(1024)S(1)} %copy-done.1, s32[8192]{0:T(1024)S(1)} %fusion.23), kind=kCustom, calls=%fused_computation.clone.1 | custom fusion | bytes 98304 | tf_op jit(solution)/shard_map/while/body/eval_jaxpr/gather | solution.py:19
  203.2 0.8 fusion.25
  204.0 24.0 %gather_fusion.2 = bf16[8192,64]{1,0:T(8,128)(2,1)S(1)} fusion(bf16[3072,64]{1,0:T(8,128)(2,1)S(1)} %get-tuple-element.181, s32[8192]{0:T(1024)S(1)} %fusion.26), kind=kCustom, calls=%fused_computation.2.clone.1 | custom fusion | bytes 2129920 | tf_op jit(solution)/shard_map/while/body/eval_jaxpr/gather | solution.py:23
  228.1 1.7 fusion.27
  230.7 37.6 %gather_fusion.1 = s32[8192]{0:T(1024)S(1)} fusion(s32[50000]{0:T(1024)} %get-tuple-element.180, s32[8192]{0:T(1024)S(1)} %fusion.23), kind=kCustom, calls=%fused_computation.1.clone.1 | custom fusion | bytes 98304 | tf_op jit(solution)/shard_map/while/body/eval_jaxpr/gather | solution.py:20
  268.2 45.5 %gather_fusion = f32[8192]{0:T(1024)S(1)} fusion(f32[50000]{0:T(1024)S(1)} %copy-done.1, s32[8192]{0:T(1024)S(1)} %fusion.23), kind=kCustom, calls=%fused_computation.clone.1 | custom fusion | bytes 98304 | tf_op jit(solution)/shard_map/while/body/eval_jaxpr/gather | solution.py:19
  313.8 0.8 fusion.25
  314.6 24.0 %gather_fusion.2 = bf16[8192,64]{1,0:T(8,128)(2,1)S(1)} fusion(bf16[3072,64]{1,0:T(8,128)(2,1)S(1)} %get-tuple-element.181, s32[8192]{0:T(1024)S(1)} %fusion.26), kind=kCustom, calls=%fused_computation.2.clone.1 | custom fusion | bytes 2129920 | tf_op jit(solution)/shard_map/while/body/eval_jaxpr/gather | solution.py:23
  338.6 1.7 fusion.27
  341.2 37.6 %gather_fusion.1 = s32[8192]{0:T(1024)S(1)} fusion(s32[50000]{0:T(1024)} %get-tuple-element.180, s32[8192]{0:T(1024)S(1)} %fusion.23), kind=kCustom, calls=%fused_computation.1.clone.1 | custom fusion | bytes 98304 | tf_op jit(solution)/shard_map/while/body/eval_jaxpr/gather | solution.py:20
  378.8 45.5 %gather_fusion = f32[8192]{0:T(1024)S(1)} fusion(f32[50000]{0:T(1024)S(1)} %copy-done.1, s32[8192]{0:T(1024)S(1)} %fusion.23), kind=kCustom, calls=%fused_computation.clone.1 | custom fusion | bytes 98304 | tf_op jit(solution)/shard_map/while/body/eval_jaxpr/gather | solution.py:19
  424.4 0.8 fusion.25
  425.2 24.0 %gather_fusion.2 = bf16[8192,64]{1,0:T(8,128)(2,1)S(1)} fusion(bf16[3072,64]{1,0:T(8,128)(2,1)S(1)} %get-tuple-element.181, s32[8192]{0:T(1024)S(1)} %fusion.26), kind=kCustom, calls=%fused_computation.2.clone.1 | custom fusion | bytes 2129920 | tf_op jit(solution)/shard_map/while/body/eval_jaxpr/gather | solution.py:23
  449.2 1.7 fusion.27
  451.8 37.6 %gather_fusion.1 = s32[8192]{0:T(1024)S(1)} fusion(s32[50000]{0:T(1024)} %get-tuple-element.180, s32[8192]{0:T(1024)S(1)} %fusion.23), kind=kCustom, calls=%fused_computation.1.clone.1 | custom fusion | bytes 98304 | tf_op jit(solution)/shard_map/while/body/eval_jaxpr/gather | solution.py:20
  489.4 45.5 %gather_fusion = f32[8192]{0:T(1024)S(1)} fusion(f32[50000]{0:T(1024)S(1)} %copy-done.1, s32[8192]{0:T(1024)S(1)} %fusion.23), kind=kCustom, calls=%fused_computation.clone.1 | custom fusion | bytes 98304 | tf_op jit(solution)/shard_map/while/body/eval_jaxpr/gather | solution.py:19
  534.9 0.8 fusion.25
  535.7 24.0 %gather_fusion.2 = bf16[8192,64]{1,0:T(8,128)(2,1)S(1)} fusion(bf16[3072,64]{1,0:T(8,128)(2,1)S(1)} %get-tuple-element.181, s32[8192]{0:T(1024)S(1)} %fusion.26), kind=kCustom, calls=%fused_computation.2.clone.1 | custom fusion | bytes 2129920 | tf_op jit(solution)/shard_map/while/body/eval_jaxpr/gather | solution.py:23
  559.8 1.7 fusion.27
  562.3 37.6 %gather_fusion.1 = s32[8192]{0:T(1024)S(1)} fusion(s32[50000]{0:T(1024)} %get-tuple-element.180, s32[8192]{0:T(1024)S(1)} %fusion.23), kind=kCustom, calls=%fused_computation.1.clone.1 | custom fusion | bytes 98304 | tf_op jit(solution)/shard_map/while/body/eval_jaxpr/gather | solution.py:20
  599.9 45.5 %gather_fusion = f32[8192]{0:T(1024)S(1)} fusion(f32[50000]{0:T(1024)S(1)} %copy-done.1, s32[8192]{0:T(1024)S(1)} %fusion.23), kind=kCustom, calls=%fused_computation.clone.1 | custom fusion | bytes 98304 | tf_op jit(solution)/shard_map/while/body/eval_jaxpr/gather | solution.py:19
  645.5 0.8 fusion.25
  646.3 24.0 %gather_fusion.2 = bf16[8192,64]{1,0:T(8,128)(2,1)S(1)} fusion(bf16[3072,64]{1,0:T(8,128)(2,1)S(1)} %get-tuple-element.181, s32[8192]{0:T(1024)S(1)} %fusion.26), kind=kCustom, calls=%fused_computation.2.clone.1 | custom fusion | bytes 2129920 | tf_op jit(solution)/shard_map/while/body/eval_jaxpr/gather | solution.py:23
  670.3 1.7 fusion.27
  672.9 37.6 %gather_fusion.1 = s32[8192]{0:T(1024)S(1)} fusion(s32[50000]{0:T(1024)} %get-tuple-element.180, s32[8192]{0:T(1024)S(1)} %fusion.23), kind=kCustom, calls=%fused_computation.1.clone.1 | custom fusion | bytes 98304 | tf_op jit(solution)/shard_map/while/body/eval_jaxpr/gather | solution.py:20
  710.5 45.5 %gather_fusion = f32[8192]{0:T(1024)S(1)} fusion(f32[50000]{0:T(1024)S(1)} %copy-done.1, s32[8192]{0:T(1024)S(1)} %fusion.23), kind=kCustom, calls=%fused_computation.clone.1 | custom fusion | bytes 98304 | tf_op jit(solution)/shard_map/while/body/eval_jaxpr/gather | solution.py:19
  756.0 0.8 fusion.25
  756.9 24.0 %gather_fusion.2 = bf16[8192,64]{1,0:T(8,128)(2,1)S(1)} fusion(bf16[3072,64]{1,0:T(8,128)(2,1)S(1)} %get-tuple-element.181, s32[8192]{0:T(1024)S(1)} %fusion.26), kind=kCustom, calls=%fused_computation.2.clone.1 | custom fusion | bytes 2129920 | tf_op jit(solution)/shard_map/while/body/eval_jaxpr/gather | solution.py:23
  780.9 1.7 fusion.27
  783.5 37.6 %gather_fusion.1 = s32[8192]{0:T(1024)S(1)} fusion(s32[50000]{0:T(1024)} %get-tuple-element.180, s32[8192]{0:T(1024)S(1)} %fusion.23), kind=kCustom, calls=%fused_computation.1.clone.1 | custom fusion | bytes 98304 | tf_op jit(solution)/shard_map/while/body/eval_jaxpr/gather | solution.py:20
  821.1 45.5 %gather_fusion = f32[8192]{0:T(1024)S(1)} fusion(f32[50000]{0:T(1024)S(1)} %copy-done.1, s32[8192]{0:T(1024)S(1)} %fusion.23), kind=kCustom, calls=%fused_computation.clone.1 | custom fusion | bytes 98304 | tf_op jit(solution)/shard_map/while/body/eval_jaxpr/gather | solution.py:19
  866.6 0.8 fusion.25
  867.4 24.0 %gather_fusion.2 = bf16[8192,64]{1,0:T(8,128)(2,1)S(1)} fusion(bf16[3072,64]{1,0:T(8,128)(2,1)S(1)} %get-tuple-element.181, s32[8192]{0:T(1024)S(1)} %fusion.26), kind=kCustom, calls=%fused_computation.2.clone.1 | custom fusion | bytes 2129920 | tf_op jit(solution)/shard_map/while/body/eval_jaxpr/gather | solution.py:23
  891.5 1.7 fusion.27
  893.4 2.4 collective-permute-start
  895.8 13.0 %copy.20 = bf16[512,64,64]{2,1,0:T(8,128)(2,1)} copy(bf16[512,64,64]{0,2,1:T(8,128)(2,1)} %param.18) | data formatting | bytes 8388608 | tf_op args[7]
  909.7 31.0 %convolution_convert_fusion.1 = bf16[1,512,64]{2,0,1:T(2,128)(2,1)S(1)} fusion(bf16[1,1023,64]{2,0,1:T(2,128)(2,1)S(1)} %copy.19, bf16[512,64,64]{2,1,0:T(8,128)(2,1)} %copy.20), kind=kOutput, calls=%fused_computation.17 | convolution fusion | flops 2147516416 | bytes 4390784 | tf_op jit(solution)/shard_map/conv_general_dilated | solution.py:53
  941.5 39.5 %all-gather.3.cloned.1.call-done = bf16[1,8192,64]{1,2,0:T(8,128)(2,1)} async-done(((bf16[1,512,64]{1,2,0:T(8,128)(2,1)}), bf16[1,8192,64]{1,2,0:T(8,128)(2,1)}) %all-gather.3.cloned.1.call-update) | async-done | bytes 1048592 | tf_op jit(solution)/shard_map/all_gather | solution.py:64
  981.0 2.1 fusion.6
  (59 shorter events, 8.4 us)
Async XLA Ops:
  6.5 974.5 %copy-start = (bf16[64,8]{0,1:T(8,128)(2,1)S(1)}, bf16[64,8]{0,1:T(8,128)(2,1)}, u32[]{:S(2)}) copy-start(bf16[64,8]{0,1:T(8,128)(2,1)} %param.19) | copy-start | bytes 3076
  6.5 974.5 %all-gather.3.cloned.1.call-start = ((), (), s32[]{:S(2)}) async-start(), calls=%async_computation | async-start | bytes 1114112 | tf_op jit(solution)/shard_map/all_gather | solution.py:64
  9.5 37.6 %copy-start.1 = (f32[50000]{0:T(1024)S(1)}, f32[50000]{0:T(1024)}, u32[]{:S(2)}) copy-start(f32[50000]{0:T(1024)} %get-tuple-element.179) | copy-start | bytes 600004 | tf_op jit(solution)/shard_map/while
  120.1 37.6 %copy-start.1 = (f32[50000]{0:T(1024)S(1)}, f32[50000]{0:T(1024)}, u32[]{:S(2)}) copy-start(f32[50000]{0:T(1024)} %get-tuple-element.179) | copy-start | bytes 600004 | tf_op jit(solution)/shard_map/while
  230.6 37.6 %copy-start.1 = (f32[50000]{0:T(1024)S(1)}, f32[50000]{0:T(1024)}, u32[]{:S(2)}) copy-start(f32[50000]{0:T(1024)} %get-tuple-element.179) | copy-start | bytes 600004 | tf_op jit(solution)/shard_map/while
  341.2 37.6 %copy-start.1 = (f32[50000]{0:T(1024)S(1)}, f32[50000]{0:T(1024)}, u32[]{:S(2)}) copy-start(f32[50000]{0:T(1024)} %get-tuple-element.179) | copy-start | bytes 600004 | tf_op jit(solution)/shard_map/while
  451.8 37.6 %copy-start.1 = (f32[50000]{0:T(1024)S(1)}, f32[50000]{0:T(1024)}, u32[]{:S(2)}) copy-start(f32[50000]{0:T(1024)} %get-tuple-element.179) | copy-start | bytes 600004 | tf_op jit(solution)/shard_map/while
  562.3 37.6 %copy-start.1 = (f32[50000]{0:T(1024)S(1)}, f32[50000]{0:T(1024)}, u32[]{:S(2)}) copy-start(f32[50000]{0:T(1024)} %get-tuple-element.179) | copy-start | bytes 600004 | tf_op jit(solution)/shard_map/while
  672.9 37.6 %copy-start.1 = (f32[50000]{0:T(1024)S(1)}, f32[50000]{0:T(1024)}, u32[]{:S(2)}) copy-start(f32[50000]{0:T(1024)} %get-tuple-element.179) | copy-start | bytes 600004 | tf_op jit(solution)/shard_map/while
  783.5 37.6 %copy-start.1 = (f32[50000]{0:T(1024)S(1)}, f32[50000]{0:T(1024)}, u32[]{:S(2)}) copy-start(f32[50000]{0:T(1024)} %get-tuple-element.179) | copy-start | bytes 600004 | tf_op jit(solution)/shard_map/while
  893.4 15.4 %collective-permute-start = (bf16[511,64]{0,1:T(8,128)(2,1)S(1)}, bf16[511,64]{0,1:T(8,128)(2,1)S(1)}, u32[]{:S(2)}, u32[]{:S(2)}) collective-permute-start(bf16[511,64]{0,1:T(8,128)(2,1)S(1)} %slice.10), channel_id=1, source_target_pairs={{0,1},{1,2},{2,3},{3,4},{4,5},{5,6},{6,7},{7,8},{8,9},{9,10},{10,1... | collective-permute-start | bytes 196232 | tf_op jit(solution)/shard_map/ppermute | solution.py:12
Sparse Core Ops, SparseCore 0:
  941.6 39.3 all-gather.2
where the time goes:
time: 992 us; the launch traced here: 990 us
  local copies, waits for them, and re-layouts  874 us (88%)
  matrix products  47 us (5%)
  waiting for transfers between devices  39.5 us (4%)
  between operations  13.4 us (1%)
  other arithmetic  12.9 us (1%)
    gather x8, local copies, waits for them, and re-layouts, block_forcing(): area = panel_area[panels]  364 us
    gather x8, local copies, waits for them, and re-layouts, block_forcing(): patch = panel_patch[panels]  301 us
    gather x8, local copies, waits for them, and re-layouts, block_forcing(): mode_rows = patch_modes[patch].astype(jnp.float32)  192 us
    all_gather x1, waiting for transfers between devices, body(): lax.all_gather(response, 'tm', axis=0, tiled=True)  39.5 us
    conv_general_dilated x1, matrix products, body(): lax.conv_general_dilated(extended[None], impulse[::-1], (1,), 'VALID', di...  31 us
  transfers between devices with their start and end apart: 2, of which 1 were waited for; matrix products, arithmetic and copies ran while one was open for 1% of the time, Pallas kernels for 0%

commit v1 on v0

v1 whole, which is shorter than its diff:
```python
import functools

import jax
import jax.numpy as jnp
from jax import lax
from jax.experimental import pallas as pl
from jax.experimental.pallas import tpu as pltpu
from jax.sharding import PartitionSpec as P

F32, BF16, I32 = jnp.float32, jnp.bfloat16, jnp.int32
GIRTH = 500
LANES = 128
HALF = 200
AREA_SCALE = 32767.0


def pow2_up(x, e, bits):
    for b in range(bits):
        x = jnp.where((e & (1 << b)) != 0, x * float(2 ** (1 << b)), x)
    return x


def pow2_down(x, bits, top):
    e = jnp.zeros(x.shape, I32)
    for b in reversed(range(bits)):
        big = x >= float(top * 2 ** ((1 << b)))
        x = jnp.where(big, x * float(2.0 ** -(1 << b)), x)
        e = e + jnp.where(big, jnp.int32(1 << b), jnp.int32(0))
    return x, e


def forcing_kernel(st_any, gi_any, cnt_any, pr_any, first_ref, second_ref, modes_any, out_ref,
                   st_ref, gi_ref, cnt_ref, pr_ref, modes_ref, sems, tab, live, rowv, colv, sel1, sel2, fv, hiv, lov, wbuf, *, group):
    steps = st_ref.shape[0]
    copies = [pltpu.make_async_copy(a, b, sems.at[i]) for i, (a, b) in enumerate((
        (st_any, st_ref), (gi_any, gi_ref), (cnt_any, cnt_ref), (pr_any, pr_ref), (modes_any, modes_ref)))]
    for c in copies:
        c.start()
    for h in range(2):
        for part, ref in enumerate((first_ref, second_ref)):
            tab[HALF * part:HALF * (part + 1), LANES * h:LANES * (h + 1)] = ref[HALF * h:HALF * (h + 1), :]
    for c in copies:
        c.wait()
    slot = lax.broadcasted_iota(I32, (LANES, LANES), 1).astype(F32)
    counts = cnt_ref[...].astype(F32)
    for j in range(steps // LANES):
        per_step = jnp.broadcast_to(counts[j:j + 1, :], (LANES, LANES)).T
        here = slice(LANES * j, LANES * (j + 1))
        live[here, :] = jnp.where(slot < per_step, pr_ref[here, :].astype(F32), 0.0)
    panel = st_ref[...] * GIRTH + gi_ref[...]
    hi = panel >> 7
    second = hi >= HALF
    rowv[...] = jnp.where(second, hi - HALF, hi)
    colv[...] = ((panel & 127) + jnp.where(second, LANES, 0)).astype(F32)

    n_groups = steps // group
    sub = lax.broadcasted_iota(I32, (8, LANES), 0)
    iota_b = lax.broadcasted_iota(I32, (256, LANES), 0).astype(F32).astype(BF16)
    iota16 = lax.broadcasted_iota(I32, (16, LANES), 0)
    one = jnp.ones((), BF16)
    zero = jnp.zeros((), BF16)

    def onehot(row_f32):
        b = jnp.broadcast_to(row_f32, (256, LANES)).astype(BF16)
        return jnp.where(iota_b == b, one, zero)

    def stage1(base):
        for p in range(group // 2):
            t0 = base + 2 * p
            oh = jnp.concatenate([onehot(colv[pl.ds(t0, 1), :]), onehot(colv[pl.ds(t0 + 1, 1), :])], axis=1)
            r = jnp.dot(tab[...], oh, preferred_element_type=F32)
            for j in range(2):
                want = jnp.broadcast_to(rowv[pl.ds(t0 + j, 1), :], (8, LANES)) - sub
                a1 = jnp.zeros((8, LANES), F32)
                a2 = jnp.zeros((8, LANES), F32)
                for v in range(HALF // 8):
                    hit = want == 8 * v
                    a1 = jnp.where(hit, r[8 * v:8 * v + 8, LANES * j:LANES * (j + 1)], a1)
                    a2 = jnp.where(hit, r[HALF + 8 * v:HALF + 8 * v + 8, LANES * j:LANES * (j + 1)], a2)
                sel1[pl.ds(t0 + j, 1), :] = jnp.sum(a1, axis=0, keepdims=True)
                sel2[pl.ds(t0 + j, 1), :] = jnp.sum(a2, axis=0, keepdims=True)

    def decode(base):
        x1 = sel1[pl.ds(base, group), :]
        x2 = sel2[pl.ds(base, group), :]
        m1, e1 = pow2_down(jnp.abs(x1), 6, 128)
        m2, e2 = pow2_down(jnp.abs(x2), 6, 128)
        qi = (m1.astype(I32) - 128) + (e1 << 7) + jnp.where(x1 < 0, 1 << 13, 0) + jnp.where(x2 < 0, 1 << 14, 0) + ((e2 & 1) << 15)
        area = qi.astype(F32) * (1.0 / AREA_SCALE)
        pa = e2 >> 1
        lov[pl.ds(base, group), :] = (m2 - 128.0) + ((pa & 1) << 7).astype(F32)
        hiv[pl.ds(base, group), :] = pa >> 1
        fv[pl.ds(base, group), :] = live[pl.ds(base, group), :] * area

    def stage2(base):
        for p in range(group // 2):
            t0 = base + 2 * p
            oh = jnp.concatenate([onehot(lov[pl.ds(t0, 1), :]), onehot(lov[pl.ds(t0 + 1, 1), :])], axis=1)
            rows = []
            zer = jnp.zeros((16, LANES), BF16)
            for j in range(2):
                f = jnp.broadcast_to(fv[pl.ds(t0 + j, 1), :], (16, LANES))
                hit = jnp.broadcast_to(hiv[pl.ds(t0 + j, 1), :], (16, LANES)) == iota16
                fm = jnp.where(hit, f, 0.0)
                fh = fm.astype(BF16)
                fl = (fm - fh.astype(F32)).astype(BF16)
                for part in (fh, fl):
                    rows.append(jnp.concatenate([part, zer] if j == 0 else [zer, part], axis=1))
            a = jnp.concatenate(rows, axis=0)
            w = lax.dot_general(a, oh, (((1,), (1,)), ((), ())), preferred_element_type=F32)
            for j in range(2):
                both = w[32 * j:32 * j + 16] + w[32 * j + 16:32 * j + 32]
                for c in range(2):
                    wbuf[c, pl.ds((t0 + j) * 16, 16), :] = both[:, LANES * c:LANES * (c + 1)]

    stage1(0)
    decode(0)

    def loop(g, c):
        base = pl.multiple_of(g * group, group)
        stage1(base + group)
        stage2(base)
        decode(base + group)
        return c

    lax.fori_loop(0, n_groups - 1, loop, 0)
    stage2((n_groups - 1) * group)

    acc = jnp.zeros((steps, modes_ref.shape[0]), F32)
    for h in range(modes_ref.shape[1] // 256):
        m = modes_ref[:, 256 * h:256 * h + 256]
        w = jnp.concatenate([wbuf.at[c][pl.ds(h, steps, 16), :] for c in range(2)], axis=1)
        wh = w.astype(BF16)
        wl = (w - wh.astype(F32)).astype(BF16)
        acc = acc + lax.dot_general(wh, m, (((1,), (1,)), ((), ())), preferred_element_type=F32)
        acc = acc + lax.dot_general(wl, m, (((1,), (1,)), ((), ())), preferred_element_type=F32)
    out_ref[...] = acc.astype(BF16)


def whole(shape):
    return pl.BlockSpec(shape, lambda i: (0,) * len(shape))


def encoded(panel_area, panel_patch):
    pad = 2 * HALF * LANES - panel_area.shape[0]
    q = (jnp.pad(panel_area, (0, pad)) * AREA_SCALE + 0.5).astype(I32)
    patch = jnp.pad(panel_patch, (0, pad))
    first = pow2_up(((q & 127) + 128).astype(F32), (q >> 7) & 63, 6)
    first = jnp.where(((q >> 13) & 1) == 1, -first, first).astype(BF16)
    second = pow2_up(((patch & 127) + 128).astype(F32), (patch >> 7) * 2 + (q >> 15), 6)
    second = jnp.where(((q >> 14) & 1) == 1, -second, second).astype(BF16)
    return first.reshape(2 * HALF, LANES), second.reshape(2 * HALF, LANES)


def forcing(wet_station, wet_girth, wet_count, pressure, panel_area, panel_patch, patch_modes, group=32):
    steps = wet_station.shape[0]
    modes = patch_modes.shape[1]
    first, second = encoded(panel_area, panel_patch)
    args = (wet_station, wet_girth, wet_count.reshape(steps // LANES, LANES), pressure, first, second, patch_modes.T)
    return pl.pallas_call(
        functools.partial(forcing_kernel, group=group),
        out_shape=jax.ShapeDtypeStruct((steps, modes), BF16),
        in_specs=[pl.BlockSpec(memory_space=pltpu.VMEM if i in (4, 5) else pltpu.HBM) for i in range(len(args))],
        out_specs=pl.BlockSpec(memory_space=pltpu.VMEM),
        scratch_shapes=[
            *[pltpu.VMEM(args[i].shape, args[i].dtype) for i in (0, 1, 2, 3, 6)],
            pltpu.SemaphoreType.DMA((5,)),
            pltpu.VMEM((2 * HALF, 256), BF16), pltpu.VMEM((steps, LANES), F32),
            pltpu.VMEM((steps, LANES), I32), pltpu.VMEM((steps, LANES), F32),
            pltpu.VMEM((steps, LANES), F32), pltpu.VMEM((steps, LANES), F32),
            pltpu.VMEM((steps, LANES), F32), pltpu.VMEM((steps, LANES), I32), pltpu.VMEM((steps, LANES), F32),
            pltpu.VMEM((2, steps * 16, LANES), F32),
        ],
        compiler_params=pltpu.CompilerParams(vmem_limit_bytes=16 * 1024 * 1024),
        cost_estimate=pl.CostEstimate(flops=2 * 10 ** 10, bytes_accessed=2 * 10 ** 6, transcendentals=0),
        name="forcing",
    )(*args)


def weights_kernel(imp_ref, out_ref, turned):
    modes = out_ref.shape[1] // 4
    quarter = imp_ref.shape[1] // 4

    def turn(m, carry):
        rows = imp_ref[pl.ds(pl.multiple_of(m * modes, modes), modes), :]
        for h in range(2):
            q = 2 * h * quarter
            block = jnp.concatenate([rows[:, q:q + quarter], rows[:, q + quarter:q + 2 * quarter]], axis=0)
            turned[h, pl.ds(pl.multiple_of(m * quarter, quarter), quarter), :] = block.astype(F32).T
        return carry

    lax.fori_loop(0, modes, turn, 0, unroll=4)

    def gather(r, carry):
        lines = [turned.at[h][pl.ds(r, modes, quarter), :].astype(BF16) for h in range(2)]
        out_ref[pl.ds(pl.multiple_of(r * modes, modes), modes), :] = jnp.concatenate(lines, axis=1)
        return carry

    lax.fori_loop(0, quarter, gather, 0, unroll=4)


def impulse_weights(impulse):
    lags, modes, _ = impulse.shape
    flat = jnp.transpose(impulse, (1, 2, 0)).reshape(modes * modes, lags)
    rows = lags // 4 * modes
    return pl.pallas_call(
        weights_kernel,
        out_shape=jax.ShapeDtypeStruct((rows, 4 * modes), BF16),
        in_specs=[pl.BlockSpec(memory_space=pltpu.VMEM)],
        out_specs=pl.BlockSpec(memory_space=pltpu.VMEM),
        scratch_shapes=[pltpu.VMEM((2, rows, 2 * modes), F32)],
        compiler_params=pltpu.CompilerParams(vmem_limit_bytes=12 * 1024 * 1024),
        cost_estimate=pl.CostEstimate(flops=10 ** 9, bytes_accessed=8 * 10 ** 6, transcendentals=0),
        name="impulse_weights",
    )(flat)


def response_kernel(early_ref, force_ref, weights, map_ref, out_ref, pair, shifts, acc):
    steps, modes = force_ref.shape
    quarter = weights.shape[0] // modes
    both = jnp.concatenate([early_ref[...], force_ref[...]], axis=0).astype(F32)
    total = both.shape[0]
    pair[0:16, :] = jnp.zeros((16, 2 * modes), F32)
    pair[16:, 0:modes] = both
    pair[0:17, modes:] = jnp.zeros((17, modes), F32)
    pair[17:16 + total, modes:] = both[:-1]
    for c in range(4):
        for i in range(2):
            d = 4 * c + 2 * i
            shifts[c, :, 128 * i:128 * i + 128] = pair[16 - d:16 - d + total, :].astype(BF16)
    first = steps - 3 * quarter
    rows = steps + 3 * quarter

    acc[...] = jnp.zeros_like(acc)

    def step(p, carry):
        top = pl.multiple_of(first - 16 * p, 16)
        left = jnp.concatenate([shifts[c, pl.ds(top, rows), :] for c in range(4)], axis=1)
        acc[...] += jnp.dot(left, weights[pl.ds(pl.multiple_of(p * 1024, 1024), 1024), :], preferred_element_type=F32)
        return carry

    lax.fori_loop(0, quarter // 16, step, 0)
    lane = lax.broadcasted_iota(I32, (steps, 2 * modes), 1) < modes
    def y(q, c):
        a = 3 * quarter - q * quarter
        return acc[a:a + steps, 128 * c:128 * c + 128]
    s = jnp.where(lane, y(0, 0), y(1, 0)) + jnp.where(lane, y(2, 1), y(3, 1))
    response = (s[:, :modes] + s[:, modes:]).astype(BF16)
    out_ref[...] = lax.dot_general(map_ref[...].reshape(-1, modes), response, (((1,), (1,)), ((), ())), preferred_element_type=F32).astype(BF16)


def local_stress(early, force, weights, whole_map):
    steps, modes = force.shape
    quarter = weights.shape[0] // modes
    owners, own = whole_map.shape[0], 8
    total = 2 * steps
    return pl.pallas_call(
        response_kernel,
        out_shape=jax.ShapeDtypeStruct((owners * own, steps), BF16),
        grid=(1,),
        in_specs=[pl.BlockSpec(memory_space=pltpu.VMEM)] * 3 + [whole((owners, own, modes))],
        out_specs=pl.BlockSpec(memory_space=pltpu.VMEM),
        scratch_shapes=[
            pltpu.VMEM((total + 16, 2 * modes), F32),
            pltpu.VMEM((4, total, 4 * modes), BF16),
            pltpu.VMEM((steps + 3 * quarter, 256), F32),
        ],
        compiler_params=pltpu.CompilerParams(vmem_limit_bytes=12 * 1024 * 1024),
        cost_estimate=pl.CostEstimate(flops=4 * 10 ** 9, bytes_accessed=4 * 10 ** 6, transcendentals=0),
        name="local_stress",
    )(early, force, weights, whole_map)


def shifted(value, axis, steps):
    count = lax.axis_size(axis)
    leading, last = (max(0, -steps), min(count, count - steps))
    return lax.ppermute(value, axis, [(source, source + steps) for source in range(leading, last)])


def body(wet_station, wet_girth, wet_count, pressure, panel_area, panel_patch, patch_modes, impulse, stress_map):
    steps = wet_station.shape[0]
    lags = impulse.shape[0]
    own_map = lax.optimization_barrier(jnp.tile(stress_map.T[None], (lax.axis_size("tm"), 1, 1)))
    whole_map = lax.all_to_all(own_map, "tm", 0, 0, tiled=True)
    weights = impulse_weights(impulse)
    force = forcing(wet_station, wet_girth, wet_count, pressure, panel_area, panel_patch, patch_modes)
    early = shifted(force, "tm", 1)
    part = local_stress(early, force, weights, whole_map)
    return lax.all_to_all(part, "tm", 0, 1, tiled=True)


def solution(mesh):
    return jax.shard_map(
        body,
        mesh=mesh,
        in_specs=(
            P(("sea", "tm"), None),
            P(("sea", "tm"), None),
            P(("sea", "tm")),
            P(("sea", "tm"), None),
            P(),
            P(),
            P(),
            P(),
            P(None, "tm"),
        ),
        out_specs=P("tm", "sea"),
        check_vma=False,
    )
```

time: 992 us -> 80.2 us (0.08)
  local copies, waits for them, and re-layouts: 874 us -> 10.7 us
  matrix products: 47 us -> 0 us
  Pallas kernels: 0 us -> 44.1 us
  waiting for transfers between devices: 39.5 us -> 0.01 us
  blocking collectives: 0 us -> 13.6 us
  between operations: 13.4 us -> 0.09 us
  other arithmetic: 12.9 us -> 1.53 us
    gather x24 -> x0, local copies, waits for them, and re-layouts: 857 us -> none  [the longest x8 364 us: block_forcing(): area = panel_area[panels]]
    pallas_call x0 -> x3, Pallas kernels: none -> 44.1 us  [the longest x1 28.9 us: forcing(): pl.pallas_call(functools.partial(forcing_kernel, group=group), out_shape=...]
    all_gather x1 -> x0, waiting for transfers between devices: 39.5 us -> none  [body(): lax.all_gather(response, 'tm', axis=0, tiled=True)]
    conv_general_dilated x1 -> x0, matrix products: 31 us -> none  [body(): lax.conv_general_dilated(extended[None], impulse[::-1], (1,), 'VALID', di...]
    dot_general x9 -> x0, matrix products: 16 us -> none  [the longest x8 13.9 us: block_forcing(): jnp.einsum('tk,tkm->tm', force, mode_rows, precision=lax.Precision.HIGHEST)]
    all_to_all x0 -> x1, blocking collectives: none -> 13.6 us  [body(): return lax.all_to_all(part, 'tm', 0, 1, tiled=True)]
  transfers between devices with their start and end apart: 2 -> 2, of which waited for: 1 -> 0; matrix products, arithmetic and copies ran while one was open for 1% -> 2% of each run, Pallas kernels for 0% -> 48%
where the time goes in v1:
time: 80.2 us; the launch traced here: 79.8 us
  Pallas kernels  44.1 us (55%)
  blocking collectives  13.6 us (17%)
  local copies, waits for them, and re-layouts  10.7 us (13%)
  starting transfers between devices  9.67 us (12%)
  other arithmetic  1.53 us (2%)
    pallas_call x1, Pallas kernels, forcing(): pl.pallas_call(functools.partial(forcing_kernel, group=group), out_shape=...  28.9 us
    all_to_all x1, blocking collectives, body(): return lax.all_to_all(part, 'tm', 0, 1, tiled=True)  13.6 us
    unnamed x19, local copies, waits for them, and re-layouts  10.1 us
    pallas_call x1, Pallas kernels, impulse_weights(): pl.pallas_call(weights_kernel, out_shape=jax.ShapeDtypeStruct((rows, 4 *...  9.37 us
    all_to_all x1, starting transfers between devices, body(): whole_map = lax.all_to_all(own_map, 'tm', 0, 0, tiled=True)  7.36 us
    pallas_call x1, Pallas kernels, local_stress(): pl.pallas_call(response_kernel, out_shape=jax.ShapeDtypeStruct((owners *...  5.88 us
    ppermute x1, starting transfers between devices, shifted(): lax.ppermute(value, axis, [(source, source + steps) for source in range(l...  2.32 us
  transfers between devices with their start and end apart: 2, of which 0 were waited for; matrix products, arithmetic and copies ran while one was open for 2% of the time, Pallas kernels for 48%

profile of v1, /device:TPU:0, one launch (start us, length us, event | category | flops | bytes accessed | tf_op | source)
XLA Modules:
  0.0 79.8 jit_solution(12915208263191576576)
XLA Ops:
  0.0 0.7 tile.2
  0.7 0.7 reshape.22
  1.4 7.4 %all-to-all-start = ((bf16[16,2,256]{2,1,0:T(2,128)(2,1)}), bf16[16,2,256]{2,1,0:T(2,128)(2,1)S(1)}, u32[]{:S(2)}, u32[]{:S(2)}) async-start(bf16[16,2,256]{2,1,0:T(2,128)(2,1)} %reshape.22), calls=%async_computation | async-start | bytes 32768 | tf_op jit(solution)/shard_map/all_to_all | solution.py:284
  8.8 1.5 %fusion.3 = (bf16[400,128]{1,0:T(8,128)(2,1)S(1)}, bf16[400,128]{1,0:T(8,128)(2,1)S(1)}) fusion(s32[50000]{0:T(1024)} %param.14, f32[50000]{0:T(1024)} %param.13), kind=kLoop, calls=%fused_computation.34 | loop fusion | flops 3840000 | bytes 604800 | tf_op jit(solution)/shard_map/reshape | solution.py:152
  10.3 0.0 copy-start.3
  10.3 1.0 %copy-done.3 = bf16[3072,64]{0,1:T(8,128)(2,1)S(1)} copy-done((bf16[3072,64]{0,1:T(8,128)(2,1)S(1)}, bf16[3072,64]{0,1:T(8,128)(2,1)}, u32[]{:S(2)}) %copy-start.3) | copy-done | bytes 393240
  11.3 0.0 copy-start.4
  11.3 0.9 %copy-done.4 = s32[512,128]{1,0:T(8,128)S(1)} copy-done((s32[512,128]{1,0:T(8,128)S(1)}, s32[512,128]{1,0:T(8,128)}, u32[]{:S(2)}) %copy-start.4) | copy-done | bytes 262168
  12.2 0.0 copy-start.5
  12.2 0.9 %copy-done.5 = s32[512,128]{1,0:T(8,128)S(1)} copy-done((s32[512,128]{1,0:T(8,128)S(1)}, s32[512,128]{1,0:T(8,128)}, u32[]{:S(2)}) %copy-start.5) | copy-done | bytes 262168
  13.2 0.0 copy-start.6
  13.2 0.9 %copy-done.6 = bf16[512,128]{1,0:T(8,128)(2,1)S(1)} copy-done((bf16[512,128]{1,0:T(8,128)(2,1)S(1)}, bf16[512,128]{1,0:T(8,128)(2,1)}, u32[]{:S(2)}) %copy-start.6) | copy-done | bytes 131096
  14.1 0.0 copy-start.7
  14.1 0.7 copy-done.7
  14.8 0.0 copy-start
  14.8 28.9 %forcing.1.force_ref = bf16[512,64]{1,0:T(8,128)(2,1)S(1)} custom-call(s32[512,128]{1,0:T(8,128)S(1)} %copy-done.4, s32[512,128]{1,0:T(8,128)S(1)} %copy-done.5, s32[4,128]{1,0:T(4,128)S(1)} %bitcast.17, bf16[512,128]{1,0:T(8,128)(2,1)S(1)} %copy-done.6, bf16[400,128]{1,0:T(8,128)(2,1)S(1)} %get-tuple-element.6.first_ref, ...), custom_call_target="tpu_custom_call" | custom-call | flops 20000000000 | bytes 2000000 | tf_op jit(solution)/shard_map/forcing/pallas_call | solution.py:160
  43.7 2.3 %collective-permute-start = (bf16[512,64]{1,0:T(8,128)(2,1)S(1)}, bf16[512,64]{1,0:T(8,128)(2,1)S(1)}, u32[]{:S(2)}, u32[]{:S(2)}) collective-permute-start(bf16[512,64]{1,0:T(8,128)(2,1)S(1)} %forcing.1.force_ref), channel_id=1, source_target_pairs={{0,1},{1,2},{2,3},{3,4},{4,5},{5,6},{6,7},{7,8},{8,9},{9,10},{10,1... | collective-permute-start | bytes 196616 | tf_op jit(solution)/shard_map/ppermute | solution.py:277
  46.0 0.0 copy-done
  46.0 9.4 %impulse_weights.1.weights = bf16[8192,256]{1,0:T(8,128)(2,1)S(1)} custom-call(bf16[4096,512]{1,0:T(8,128)(2,1)S(1)} %bitcast.14), custom_call_target="tpu_custom_call" | custom-call | flops 1000000000 | bytes 8000000 | tf_op jit(solution)/shard_map/impulse_weights/pallas_call | solution.py:206
  55.4 0.0 copy-start.1
  55.4 1.9 %copy-done.1 = bf16[8192,256]{1,0:T(8,128)(2,1)} copy-done((bf16[8192,256]{1,0:T(8,128)(2,1)}, bf16[8192,256]{1,0:T(8,128)(2,1)S(1)}, u32[]{:S(2)}) %copy-start.1) | copy-done | bytes 4194328
  57.3 0.0 all-to-all-done
  57.3 0.1 reshape.23.map_ref
  57.4 0.0 collective-permute-done.early_ref
  57.5 0.0 copy-start.2
  57.5 2.2 %copy-done.2 = bf16[8192,256]{1,0:T(8,128)(2,1)S(1)} copy-done((bf16[8192,256]{1,0:T(8,128)(2,1)S(1)}, bf16[8192,256]{1,0:T(8,128)(2,1)}, u32[]{:S(2)}) %copy-start.2) | copy-done | bytes 4194328
  59.6 5.9 %local_stress.1 = bf16[128,512]{1,0:T(8,128)(2,1)S(1)} custom-call(bf16[512,64]{1,0:T(8,128)(2,1)S(1)} %collective-permute-done.early_ref, bf16[512,64]{1,0:T(8,128)(2,1)S(1)} %forcing.1.force_ref, bf16[8192,256]{1,0:T(8,128)(2,1)S(1)} %copy-done.2, bf16[16,8,64]{2,1,0:T(8,128)(2,1)S(1)} %reshape.23.map_ref), custom_call_target="tpu_custom_call" | custom-call | flops 4000000000 | bytes 4000000 | tf_op jit(solution)/shard_map/local_stress/pallas_call | solution.py:257
  65.5 13.6 %all_to_all.24 = bf16[16,8,512]{2,1,0:T(8,128)(2,1)S(1)} all-to-all(bf16[16,8,512]{2,1,0:T(8,128)(2,1)S(1)} %bitcast.15), channel_id=1, replica_groups=mesh['sea'=2,'tm'=16] {'tm'}, dimensions={0} | all-to-all | bytes 262144 | tf_op jit(solution)/shard_map/all_to_all | solution.py:289
  79.1 0.7 copy.11
Async XLA Ops:
  1.4 56.0 %all-to-all-start = ((bf16[16,2,256]{2,1,0:T(2,128)(2,1)}), bf16[16,2,256]{2,1,0:T(2,128)(2,1)S(1)}, u32[]{:S(2)}, u32[]{:S(2)}) async-start(bf16[16,2,256]{2,1,0:T(2,128)(2,1)} %reshape.22), calls=%async_computation | async-start | bytes 32768 | tf_op jit(solution)/shard_map/all_to_all | solution.py:284
  10.3 1.0 %copy-start.3 = (bf16[3072,64]{0,1:T(8,128)(2,1)S(1)}, bf16[3072,64]{0,1:T(8,128)(2,1)}, u32[]{:S(2)}) copy-start(bf16[3072,64]{0,1:T(8,128)(2,1)} %param.15) | copy-start | bytes 1179652
  11.3 0.9 %copy-start.4 = (s32[512,128]{1,0:T(8,128)S(1)}, s32[512,128]{1,0:T(8,128)}, u32[]{:S(2)}) copy-start(s32[512,128]{1,0:T(8,128)} %st_any.1) | copy-start | bytes 786436
  12.2 0.9 %copy-start.5 = (s32[512,128]{1,0:T(8,128)S(1)}, s32[512,128]{1,0:T(8,128)}, u32[]{:S(2)}) copy-start(s32[512,128]{1,0:T(8,128)} %gi_any.1) | copy-start | bytes 786436
  13.2 0.9 %copy-start.6 = (bf16[512,128]{1,0:T(8,128)(2,1)S(1)}, bf16[512,128]{1,0:T(8,128)(2,1)}, u32[]{:S(2)}) copy-start(bf16[512,128]{1,0:T(8,128)(2,1)} %pr_any.1) | copy-start | bytes 393220
  14.1 0.7 copy-start.7
  14.8 31.2 %copy-start = (bf16[512,64,64]{0,2,1:T(8,128)(2,1)S(1)}, bf16[512,64,64]{0,2,1:T(8,128)(2,1)}, u32[]{:S(2)}) copy-start(bf16[512,64,64]{0,2,1:T(8,128)(2,1)} %param.16) | copy-start | bytes 12582916
  43.7 13.8 %collective-permute-start = (bf16[512,64]{1,0:T(8,128)(2,1)S(1)}, bf16[512,64]{1,0:T(8,128)(2,1)S(1)}, u32[]{:S(2)}, u32[]{:S(2)}) collective-permute-start(bf16[512,64]{1,0:T(8,128)(2,1)S(1)} %forcing.1.force_ref), channel_id=1, source_target_pairs={{0,1},{1,2},{2,3},{3,4},{4,5},{5,6},{6,7},{7,8},{8,9},{9,10},{10,1... | collective-permute-start | bytes 196616 | tf_op jit(solution)/shard_map/ppermute | solution.py:277
  55.4 2.0 %copy-start.1 = (bf16[8192,256]{1,0:T(8,128)(2,1)}, bf16[8192,256]{1,0:T(8,128)(2,1)S(1)}, u32[]{:S(2)}) copy-start(bf16[8192,256]{1,0:T(8,128)(2,1)S(1)} %impulse_weights.1.weights) | copy-start | bytes 12582916
  57.5 2.2 %copy-start.2 = (bf16[8192,256]{1,0:T(8,128)(2,1)S(1)}, bf16[8192,256]{1,0:T(8,128)(2,1)}, u32[]{:S(2)}) copy-start(bf16[8192,256]{1,0:T(8,128)(2,1)} %copy-done.1) | copy-start | bytes 12582916

commit v2 on v0

v2 whole, which is shorter than its diff:
```python
import functools

import jax
import jax.numpy as jnp
from jax import lax
from jax.experimental import pallas as pl
from jax.experimental.pallas import tpu as pltpu
from jax.sharding import PartitionSpec as P

F32, BF16, I32 = jnp.float32, jnp.bfloat16, jnp.int32
GIRTH = 500
LANES = 128
HALF = 200
AREA_SCALE = 32767.0


def pow2_up(x, e, bits):
    for b in range(bits):
        x = jnp.where((e & (1 << b)) != 0, x * float(2 ** (1 << b)), x)
    return x


def pow2_down(x, bits, top):
    e = jnp.zeros(x.shape, I32)
    for b in reversed(range(bits)):
        big = x >= float(top * 2 ** ((1 << b)))
        x = jnp.where(big, x * float(2.0 ** -(1 << b)), x)
        e = e + jnp.where(big, jnp.int32(1 << b), jnp.int32(0))
    return x, e


def shuffled(x, sub):
    x = list(x)
    for k in (1, 2, 4):
        keep = (sub & k) == 0
        for i in range(8):
            if i & k == 0:
                u, v = x[i], x[i | k]
                x[i] = jnp.where(keep, u, pltpu.roll(v, k, 0))
                x[i | k] = jnp.where(keep, pltpu.roll(u, 8 - k, 0), v)
    return x


def forcing_kernel(st_any, gi_any, cnt_any, pr_any, modes_any, first_ref, second_ref, out_ref,
                   st_ref, gi_ref, cnt_ref, pr_ref, modes_ref, sems, tab, xs, sc, sr, sp,
                   pc, prow, pp, sel1, sel2, fhv, flv, hiv, lov, wt, rankc):
    steps = st_ref.shape[0]
    modes = modes_ref.shape[0]
    blocks = steps // LANES
    copies = [pltpu.make_async_copy(x, y, sems.at[i]) for i, (x, y) in enumerate((
        (cnt_any, cnt_ref), (st_any, st_ref), (gi_any, gi_ref), (pr_any, pr_ref), (modes_any, modes_ref)))]
    for c in copies:
        c.start()
    for h in range(2):
        for part, ref in enumerate((first_ref, second_ref)):
            tab[HALF * part:HALF * (part + 1), LANES * h:LANES * (h + 1)] = ref[HALF * h:HALF * (h + 1), :]
    sub = lax.broadcasted_iota(I32, (8, LANES), 0)
    slot = lax.broadcasted_iota(I32, (LANES, LANES), 1).astype(F32)
    line = lax.broadcasted_iota(I32, (LANES, LANES), 0).astype(F32)
    copies[0].wait()
    counts = cnt_ref[...].astype(F32)
    n64 = jnp.sum(jnp.where(counts > 64.0, 1.0, 0.0)).astype(I32)
    n32 = jnp.sum(jnp.where(counts > 32.0, 1.0, 0.0)).astype(I32)
    lane_row = lax.broadcasted_iota(I32, (1, LANES), 1).astype(F32)
    count_row = [counts[j:j + 1, :] for j in range(blocks)]
    key_row = [count_row[j] * float(steps) + (float(steps - 1 - LANES * j) - lane_row) for j in range(blocks)]
    count_col = [jnp.broadcast_to(count_row[j], (LANES, LANES)).T for j in range(blocks)]
    key_col = [count_col[j] * float(steps) + (float(steps - 1 - LANES * j) - line) for j in range(blocks)]
    rank_row = []
    for j in range(blocks):
        above = jnp.zeros((8, LANES), F32)
        for i in range(blocks):
            for v in range(LANES // 8):
                above = above + jnp.where(key_col[i][8 * v:8 * v + 8] > key_row[j], 1.0, 0.0)
        rank_row.append(jnp.sum(above, axis=0, keepdims=True))
        rankc[LANES * j:LANES * (j + 1), :] = jnp.broadcast_to(rank_row[j], (LANES, LANES)).T
    for c in copies[1:4]:
        c.wait()
    for j in range(blocks):
        here = slice(LANES * j, LANES * (j + 1))
        panel = st_ref[here, :] * GIRTH + gi_ref[here, :]
        hi = panel >> 7
        second = hi >= HALF
        xs[here, 0:LANES] = ((panel & 127) + jnp.where(second, LANES, 0)).astype(F32).astype(BF16)
        xs[here, LANES:2 * LANES] = jnp.where(second, hi - HALF, hi).astype(F32).astype(BF16)
        xs[here, 2 * LANES:] = jnp.where(slot < count_col[j], pr_ref[here, :].astype(F32), 0.0).astype(BF16)
    for j in range(blocks):
        here = slice(LANES * j, LANES * (j + 1))
        place = jnp.concatenate([jnp.where(rank_row[i] == line + float(LANES * j), 1.0, 0.0).astype(BF16) for i in range(blocks)], axis=1)
        y = jnp.dot(place, xs[...], preferred_element_type=F32)
        for i, ref in enumerate((sc, sr, sp)):
            ref[here, :] = y[:, LANES * i:LANES * (i + 1)]
    for ref in (sc, sr, sp):
        ref[steps:, :] = jnp.zeros((LANES, LANES), F32)

    group = LANES // 4
    n_full = (n64 + (group - 1)) // group
    base2 = n_full * group
    n_half = (jnp.maximum(n32 - base2, 0) + (2 * group - 1)) // (2 * group)
    base4 = base2 + n_half * 2 * group
    n_quarter = (jnp.maximum(steps - base4, 0) + (4 * group - 1)) // (4 * group)
    n_all = n_full + n_half + n_quarter
    firsts = {1: (n_full, 0, 0), 2: (n_half, base2, n_full), 4: (n_quarter, base4, n_full + n_half)}
    lane = lax.broadcasted_iota(I32, (group, LANES), 1)

    for pack, (n, start, where) in firsts.items():
        def gather(g, carry, pack=pack, start=start, where=where):
            source = start + g * (group * pack)
            target = pl.multiple_of((where + g) * group, group)
            for s_ref, p_ref in ((sc, pc), (sr, prow), (sp, pp)):
                x = s_ref[pl.ds(pl.multiple_of(source, group), group), :]
                for c in range(1, pack):
                    y = s_ref[pl.ds(pl.multiple_of(source + group * c, group), group), :]
                    x = jnp.where(lane < LANES // pack * c, x, pltpu.roll(y, LANES // pack * c, 1))
                p_ref[pl.ds(target, group), :] = x
            return carry
        lax.fori_loop(0, n, gather, 0)

    iota_b = lax.broadcasted_iota(I32, (256, LANES), 0).astype(F32).astype(BF16)
    one = jnp.ones((), BF16)
    zero = jnp.zeros((), BF16)

    def onehot(row_f32, depth):
        b = jnp.broadcast_to(row_f32, (depth, LANES)).astype(BF16)
        return jnp.where(iota_b[:depth] == b, one, zero)

    def stage1_pair(t0):
        oh = jnp.concatenate([onehot(pc[pl.ds(t0 + j, 1), :], 256) for j in range(2)], axis=1)
        r = jnp.dot(tab[...], oh, preferred_element_type=F32)
        for j in range(2):
            want = jnp.broadcast_to(prow[pl.ds(t0 + j, 1), :].astype(I32), (8, LANES)) - sub
            a1 = jnp.zeros((8, LANES), F32)
            a2 = jnp.zeros((8, LANES), F32)
            for v in range(HALF // 8):
                hit = want == 8 * v
                a1 = jnp.where(hit, r[8 * v:8 * v + 8, LANES * j:LANES * (j + 1)], a1)
                a2 = jnp.where(hit, r[HALF + 8 * v:HALF + 8 * v + 8, LANES * j:LANES * (j + 1)], a2)
            sel1[pl.ds(t0 + j, 1), :] = jnp.sum(a1, axis=0, keepdims=True)
            sel2[pl.ds(t0 + j, 1), :] = jnp.sum(a2, axis=0, keepdims=True)

    def decode(base, count):
        here = pl.ds(base, count)
        x1 = sel1[here, :]
        x2 = sel2[here, :]
        m1, e1 = pow2_down(jnp.abs(x1), 6, 128)
        m2, e2 = pow2_down(jnp.abs(x2), 6, 128)
        qi = (m1.astype(I32) - 128) + (e1 << 7) + jnp.where(x1 < 0, 1 << 13, 0) + jnp.where(x2 < 0, 1 << 14, 0) + ((e2 & 1) << 15)
        f = pp[here, :] * (qi.astype(F32) * (1.0 / AREA_SCALE))
        high = f.astype(BF16).astype(F32)
        fhv[here, :] = high
        flv[here, :] = f - high
        lov[here, :] = m2 - 128.0
        hiv[here, :] = e2 >> 1

    sel1[0:group, :] = jnp.full((group, LANES), 128.0, F32)
    sel2[0:group, :] = jnp.full((group, LANES), 128.0, F32)

    def lookup(g, carry):
        before = pl.multiple_of(jnp.maximum(g - 1, 0) * group, group)
        base = pl.multiple_of(g * group, group)
        for p in range(group // 2):
            stage1_pair(base + 2 * p)
            if p % 4 == 1:
                decode(pl.multiple_of(before + 8 * (p // 4), 8), 8)
        return carry

    lax.fori_loop(0, n_all, lookup, 0)
    decode(pl.multiple_of((n_all - 1) * group, group), group)


    high_parts = wt.shape[0]
    iota_h = lax.broadcasted_iota(I32, (high_parts, LANES), 0)
    chunk_lane = lax.broadcasted_iota(I32, (2 * high_parts, LANES), 1)

    for pack, (n, start, where) in firsts.items():
        def scatter(g, carry, pack=pack, start=start, where=where):
            packed = (where + g) * group
            place = start + g * (group * pack)
            for o in range(group // 8):
                sums = [[None] * 8 for _ in range(pack)]
                for p in range(4):
                    rows = []
                    hots = []
                    for j in range(2):
                        t = pl.ds(packed + 8 * o + 2 * p + j, 1)
                        hots.append(onehot(lov[t, :], LANES))
                        hit = jnp.broadcast_to(hiv[t, :], (high_parts, LANES)) == iota_h
                        high = jnp.where(hit, jnp.broadcast_to(fhv[t, :], (high_parts, LANES)), 0.0)
                        low = jnp.where(hit, jnp.broadcast_to(flv[t, :], (high_parts, LANES)), 0.0)
                        both = jnp.concatenate([high, low], axis=0)
                        for c in range(pack):
                            if pack > 1:
                                width = LANES // pack
                                mine = jnp.where((chunk_lane >= width * c) & (chunk_lane < width * (c + 1)), both, 0.0)
                            else:
                                mine = both
                            mine = mine.astype(BF16)
                            none = jnp.zeros_like(mine)
                            rows.append(jnp.concatenate([mine, none] if j == 0 else [none, mine], axis=1))
                    w = lax.dot_general(jnp.concatenate(rows, axis=0), jnp.concatenate(hots, axis=1),
                                        (((1,), (1,)), ((), ())), preferred_element_type=F32)
                    for j in range(2):
                        for c in range(pack):
                            at = 2 * high_parts * (j * pack + c)
                            sums[c][2 * p + j] = w[at:at + high_parts] + w[at + high_parts:at + 2 * high_parts]
                for c in range(pack):
                    spot = pl.ds(pl.multiple_of(place + group * c + 8 * o, 8), 8)
                    for hb in range(high_parts // 8):
                        for i, x in enumerate(shuffled([y[8 * hb:8 * hb + 8] for y in sums[c]], sub)):
                            wt[8 * hb + i, spot, :] = x
            return carry
        lax.fori_loop(0, n, scatter, 0)

    copies[4].wait()
    ordered = []
    for j in range(blocks):
        here = slice(LANES * j, LANES * (j + 1))
        acc = jnp.zeros((2 * LANES, modes), F32)
        for h in range(high_parts // 2):
            w = jnp.concatenate([wt[2 * h, here, :], wt[2 * h + 1, here, :]], axis=1)
            wh = w.astype(BF16)
            wl = (w - wh.astype(F32)).astype(BF16)
            acc = acc + lax.dot_general(jnp.concatenate([wh, wl], axis=0), modes_ref[:, 256 * h:256 * h + 256],
                                        (((1,), (1,)), ((), ())), preferred_element_type=F32)
        ordered.append((acc[:LANES] + acc[LANES:]).astype(BF16))
    ordered = jnp.concatenate(ordered, axis=0)
    for j in range(blocks):
        here = slice(LANES * j, LANES * (j + 1))
        back = jnp.concatenate([jnp.where(rankc[here, :] == slot + float(LANES * i), 1.0, 0.0).astype(BF16) for i in range(blocks)], axis=1)
        out_ref[here, :] = jnp.dot(back, ordered, preferred_element_type=F32).astype(BF16)


def whole(shape):
    return pl.BlockSpec(shape, lambda i: (0,) * len(shape))


def encoded(panel_area, panel_patch):
    pad = 2 * HALF * LANES - panel_area.shape[0]
    q = (jnp.pad(panel_area, (0, pad)) * AREA_SCALE + 0.5).astype(I32)
    patch = jnp.pad(panel_patch, (0, pad))
    first = pow2_up(((q & 127) + 128).astype(F32), (q >> 7) & 63, 6)
    first = jnp.where(((q >> 13) & 1) == 1, -first, first).astype(BF16)
    second = pow2_up(((patch & 127) + 128).astype(F32), (patch >> 7) * 2 + (q >> 15), 6)
    second = jnp.where(((q >> 14) & 1) == 1, -second, second).astype(BF16)
    return first.reshape(2 * HALF, LANES), second.reshape(2 * HALF, LANES)


def forcing(wet_station, wet_girth, wet_count, pressure, panel_area, panel_patch, patch_modes):
    steps = wet_station.shape[0]
    patches, modes = patch_modes.shape
    first, second = encoded(panel_area, panel_patch)
    far = (wet_station, wet_girth, wet_count.reshape(steps // LANES, LANES), pressure, patch_modes.T)
    far = tuple(pltpu.with_memory_space_constraint(x, pltpu.HBM) for x in far)
    table = lambda n, t: pltpu.VMEM((n, LANES), t)
    return pl.pallas_call(
        forcing_kernel,
        out_shape=jax.ShapeDtypeStruct((steps, modes), BF16),
        in_specs=[pl.BlockSpec(memory_space=pltpu.HBM)] * 5 + [pl.BlockSpec(memory_space=pltpu.VMEM)] * 2,
        out_specs=pl.BlockSpec(memory_space=pltpu.VMEM),
        scratch_shapes=[
            *[pltpu.VMEM(x.shape, x.dtype) for x in far],
            pltpu.SemaphoreType.DMA((5,)),
            pltpu.VMEM((2 * HALF, 256), BF16),
            pltpu.VMEM((steps, 3 * LANES), BF16),
            *[table(steps + LANES, F32)] * 3,
            *[table(steps, F32)] * 7,
            table(steps, I32), table(steps, F32),
            pltpu.VMEM((patches // LANES, steps + LANES, LANES), F32),
            table(steps, F32),
        ],
        compiler_params=pltpu.CompilerParams(vmem_limit_bytes=24 * 1024 * 1024),
        cost_estimate=pl.CostEstimate(flops=2 * 10 ** 10, bytes_accessed=2 * 10 ** 6, transcendentals=0),
        name="forcing",
    )(*far, first, second)


def weights_kernel(imp_ref, out_ref):
    modes = out_ref.shape[1] // 4
    quarter = imp_ref.shape[1] // 4
    row = lax.broadcasted_iota(I32, (2 * quarter, 2 * quarter), 0)
    col = lax.broadcasted_iota(I32, (2 * quarter, 2 * quarter), 1)
    order = jnp.where(((row >> 3) & 1) * quarter + (row >> 4) * 8 + (row & 7) == col, 1.0, 0.0).astype(BF16)

    def turn(i, carry):
        pair = [imp_ref[pl.ds(pl.multiple_of((2 * i + m) * modes, modes), modes), :] for m in range(2)]
        block = jnp.concatenate([jnp.concatenate([x[:, quarter * q:quarter * (q + 1)] for x in pair], axis=1) for q in range(4)], axis=0)
        y = lax.dot_general(order, block, (((1,), (1,)), ((), ())), preferred_element_type=F32).astype(BF16)
        for v in range(quarter // 8):
            out_ref[pl.ds(pl.multiple_of(v * (8 * modes) + 16 * i, 16), 16), :] = y[16 * v:16 * v + 16]
        return carry

    lax.fori_loop(0, modes // 2, turn, 0, unroll=8)


def impulse_weights(impulse):
    lags, modes, _ = impulse.shape
    flat = jnp.transpose(impulse, (1, 2, 0)).reshape(modes * modes, lags)
    return pl.pallas_call(
        weights_kernel,
        out_shape=jax.ShapeDtypeStruct((lags // 4 * modes, 4 * modes), BF16),
        in_specs=[pl.BlockSpec(memory_space=pltpu.VMEM)],
        out_specs=pl.BlockSpec(memory_space=pltpu.VMEM),
        compiler_params=pltpu.CompilerParams(vmem_limit_bytes=8 * 1024 * 1024),
        cost_estimate=pl.CostEstimate(flops=3 * 10 ** 9, bytes_accessed=8 * 10 ** 6, transcendentals=0),
        name="impulse_weights",
    )(flat)


def products(seq, wts, pair, x8, shifts, acc):
    count, modes = seq.shape
    depth = 16 * modes
    steps = wts.shape[0] // depth
    quarter = 16 * steps
    pair[0:8, :] = jnp.zeros((8, 2 * modes), F32)
    pair[8:, 0:modes] = seq
    pair[0:9, modes:] = jnp.zeros((9, modes), F32)
    pair[9:8 + count, modes:] = seq[:-1]
    for i in range(4):
        x8[:, 2 * modes * i:2 * modes * (i + 1)] = pair[8 - 2 * i:8 - 2 * i + count, :].astype(BF16)
    row = lax.broadcasted_iota(I32, (8 * modes, 8 * modes), 0)
    col = lax.broadcasted_iota(I32, (8 * modes, 8 * modes), 1)
    spread = jnp.where((row & (modes - 1)) * 8 + row // modes == col, 1.0, 0.0).astype(BF16)
    last = jnp.zeros((8, 8 * modes), F32)
    for k in range(count // LANES):
        here = slice(LANES * k, LANES * (k + 1))
        y = jnp.dot(x8[here, :], spread, preferred_element_type=F32)
        shifts[here, 0:8 * modes] = y.astype(BF16)
        shifts[here, 8 * modes:] = jnp.concatenate([last, y[:-8]], axis=0).astype(BF16)
        last = y[-8:]
    cut = depth // 2
    halves = [None, None]
    for p in range(steps):
        left = shifts[quarter - 16 * p:count - 16 * p, :]
        for i in range(2):
            part = jnp.dot(left[:, cut * i:cut * (i + 1)], wts[depth * p + cut * i:depth * p + cut * (i + 1), :], preferred_element_type=F32)
            halves[i] = part if p == 0 else halves[i] + part
    acc[...] = halves[0] + halves[1]


def stress_kernel(early_ref, force_ref, map_ref, wts, out_ref, pair, x8, shifts, acc):
    steps, modes = force_ref.shape
    quarter = wts.shape[0] // modes
    seq = jnp.concatenate([early_ref[...], force_ref[...]], axis=0).astype(F32)
    products(seq, wts, pair, x8, shifts, acc)

    def y(q):
        return acc[(3 - q) * quarter:(3 - q) * quarter + steps, 128 * (q // 2):128 * (q // 2) + 128]

    lane = lax.broadcasted_iota(I32, (steps, 2 * modes), 1) < modes
    s = jnp.where(lane, y(0), y(1)) + jnp.where(lane, y(2), y(3))
    response = (s[:, :modes] + s[:, modes:]).astype(BF16)
    flat = map_ref[...].reshape(-1, map_ref.shape[2])
    lines, folds = flat.shape[0], flat.shape[1] // modes
    parts = jnp.concatenate([flat[:, modes * b:modes * (b + 1)] for b in range(folds)], axis=0)
    row = lax.broadcasted_iota(I32, (lines * folds, lines * folds), 0)
    col = lax.broadcasted_iota(I32, (lines * folds, lines * folds), 1)
    order = jnp.where((row & (folds - 1)) * lines + row // folds == col, 1.0, 0.0).astype(BF16)
    hot_map = jnp.dot(order, parts, preferred_element_type=F32).astype(BF16)
    out_ref[...] = lax.dot_general(hot_map, response, (((1,), (1,)), ((), ())), preferred_element_type=F32).astype(BF16)


def work(count, modes):
    return [
        pltpu.VMEM((count + 8, 2 * modes), F32),
        pltpu.VMEM((count, 8 * modes), BF16),
        pltpu.VMEM((count, 16 * modes), BF16),
    ]


def local_stress(early, force, whole_map, weights):
    steps, modes = force.shape
    quarter = weights.shape[0] // modes
    hot = whole_map.size // modes
    return pl.pallas_call(
        stress_kernel,
        out_shape=jax.ShapeDtypeStruct((hot, steps), BF16),
        in_specs=[pl.BlockSpec(memory_space=pltpu.VMEM)] * 4,
        out_specs=pl.BlockSpec(memory_space=pltpu.VMEM),
        scratch_shapes=[*work(2 * steps, modes), pltpu.VMEM((2 * steps - quarter, 4 * modes), F32)],
        compiler_params=pltpu.CompilerParams(vmem_limit_bytes=20480 * 1024),
        cost_estimate=pl.CostEstimate(flops=4 * 10 ** 9, bytes_accessed=5 * 10 ** 6, transcendentals=0),
        name="local_stress",
    )(early, force, whole_map, weights)


def shifted(value, axis, steps):
    count = lax.axis_size(axis)
    leading, last = (max(0, -steps), min(count, count - steps))
    return lax.ppermute(value, axis, [(source, source + steps) for source in range(leading, last)])


def body(wet_station, wet_girth, wet_count, pressure, panel_area, panel_patch, patch_modes, impulse, stress_map):
    steps = wet_station.shape[0]
    own_map = jnp.tile(stress_map.T.reshape(1, -1, 256), (lax.axis_size("tm"), 1, 1))
    whole_map = lax.all_to_all(own_map, "tm", 0, 0, tiled=True)
    force = forcing(wet_station, wet_girth, wet_count, pressure, panel_area, panel_patch, patch_modes)
    force, whole_map = lax.optimization_barrier((force, whole_map))
    early = shifted(force, "tm", 1)
    weights = pltpu.with_memory_space_constraint(impulse_weights(impulse), pltpu.VMEM)
    part = local_stress(early, force, whole_map, weights)
    return lax.all_to_all(part, "tm", 0, 1, tiled=True)


def solution(mesh):
    return jax.shard_map(
        body,
        mesh=mesh,
        in_specs=(
            P(("sea", "tm"), None),
            P(("sea", "tm"), None),
            P(("sea", "tm")),
            P(("sea", "tm"), None),
            P(),
            P(),
            P(),
            P(),
            P(None, "tm"),
        ),
        out_specs=P("tm", "sea"),
        check_vma=False,
    )
```

time: 992 us -> 59.7 us (0.06)
  local copies, waits for them, and re-layouts: 874 us -> 4.22 us
  matrix products: 47 us -> 0 us
  waiting for transfers between devices: 39.5 us -> 0.01 us
  Pallas kernels: 0 us -> 28.7 us
  blocking collectives: 0 us -> 13.6 us
  between operations: 13.4 us -> 0.07 us
  other arithmetic: 12.9 us -> 1.53 us
    gather x24 -> x0, local copies, waits for them, and re-layouts: 857 us -> none  [the longest x8 364 us: block_forcing(): area = panel_area[panels]]
    all_gather x1 -> x0, waiting for transfers between devices: 39.5 us -> none  [body(): lax.all_gather(response, 'tm', axis=0, tiled=True)]
    conv_general_dilated x1 -> x0, matrix products: 31 us -> none  [body(): lax.conv_general_dilated(extended[None], impulse[::-1], (1,), 'VALID', di...]
    pallas_call x0 -> x3, Pallas kernels: none -> 28.7 us  [the longest x1 21.7 us: forcing(): pl.pallas_call(forcing_kernel, out_shape=jax.ShapeDtypeStruct((steps, mod...]
    dot_general x9 -> x0, matrix products: 16 us -> none  [the longest x8 13.9 us: block_forcing(): jnp.einsum('tk,tkm->tm', force, mode_rows, precision=lax.Precision.HIGHEST)]
    all_to_all x0 -> x1, blocking collectives: none -> 13.6 us  [body(): return lax.all_to_all(part, 'tm', 0, 1, tiled=True)]
    unnamed x3, local copies, waits for them, and re-layouts: 13 us -> 2.84 us
  transfers between devices with their start and end apart: 2 -> 2, of which waited for: 1 -> 0; matrix products, arithmetic and copies ran while one was open for 1% -> 3% of each run, Pallas kernels for 0% -> 40%
where the time goes in v2:
time: 59.7 us; the launch traced here: 59.4 us
  Pallas kernels  28.7 us (48%)
  blocking collectives  13.6 us (23%)
  starting transfers between devices  11.2 us (19%)
  local copies, waits for them, and re-layouts  4.22 us (7%)
  other arithmetic  1.53 us (3%)
    pallas_call x1, Pallas kernels, forcing(): pl.pallas_call(forcing_kernel, out_shape=jax.ShapeDtypeStruct((steps, mod...  21.7 us
    all_to_all x1, blocking collectives, body(): return lax.all_to_all(part, 'tm', 0, 1, tiled=True)  13.6 us
    all_to_all x1, starting transfers between devices, body(): whole_map = lax.all_to_all(own_map, 'tm', 0, 0, tiled=True)  7.36 us
    pallas_call x1, Pallas kernels, local_stress(): pl.pallas_call(stress_kernel, out_shape=jax.ShapeDtypeStruct((hot, steps)...  4.94 us
    ppermute x1, starting transfers between devices, shifted(): lax.ppermute(value, axis, [(source, source + steps) for source in range(l...  3.86 us
    unnamed x3, local copies, waits for them, and re-layouts  2.84 us
    pallas_call x1, Pallas kernels, impulse_weights(): pl.pallas_call(weights_kernel, out_shape=jax.ShapeDtypeStruct((lags // 4...  2.05 us
    reshape x1, other arithmetic, encoded(): return (first.reshape(2 * HALF, LANES), second.reshape(2 * HALF, LANES))  1.53 us
  transfers between devices with their start and end apart: 2, of which 0 were waited for; matrix products, arithmetic and copies ran while one was open for 3% of the time, Pallas kernels for 40%

profile of v2, /device:TPU:0, one launch (start us, length us, event | category | flops | bytes accessed | tf_op | source)
XLA Modules:
  0.0 59.4 jit_solution(13675050970120156534)
XLA Ops:
  0.0 0.8 %tile.8 = bf16[2,256]{1,0:T(2,128)(2,1)S(1)} reshape(bf16[8,64]{1,0:T(8,128)(2,1)} %bitcast.17) | data formatting | bytes 2048 | tf_op jit(solution)/shard_map/tile | solution.py:394
  0.8 0.6 %tile.9 = bf16[16,2,256]{2,1,0:T(2,128)(2,1)} broadcast(bf16[2,256]{1,0:T(2,128)(2,1)S(1)} %tile.8), dimensions={1,2} | broadcast | bytes 17408 | tf_op jit(solution)/shard_map/tile | solution.py:394
  1.4 7.4 %all-to-all-start = ((bf16[16,2,256]{2,1,0:T(2,128)(2,1)}), bf16[16,2,256]{2,1,0:T(2,128)(2,1)S(1)}, u32[]{:S(2)}, u32[]{:S(2)}) async-start(bf16[16,2,256]{2,1,0:T(2,128)(2,1)} %tile.9), calls=%async_computation | async-start | bytes 32768 | tf_op jit(solution)/shard_map/all_to_all | solution.py:395
  8.7 1.5 %fusion.3 = (bf16[400,128]{1,0:T(8,128)(2,1)S(1)}, bf16[400,128]{1,0:T(8,128)(2,1)S(1)}) fusion(s32[50000]{0:T(1024)} %param.14, f32[50000]{0:T(1024)} %param.13), kind=kLoop, calls=%fused_computation.34 | loop fusion | flops 3840000 | bytes 604800 | tf_op jit(solution)/shard_map/reshape | solution.py:245
  10.3 21.7 %forcing.1.force_ref = bf16[512,64]{1,0:T(8,128)(2,1)S(1)} custom-call(s32[512,128]{1,0:T(8,128)} %st_any.1, s32[512,128]{1,0:T(8,128)} %gi_any.1, s32[4,128]{1,0:T(4,128)} %bitcast.19, bf16[512,128]{1,0:T(8,128)(2,1)} %pr_any.1, bf16[64,3072]{1,0:T(8,128)(2,1)} %bitcast.18, bf16[400,128]{1,0:T(8,128)(2,1)S(1)} %get-tuple-element.10.first_ref, ...), custom_call_target="tpu_custom_call" | custom-call | flops 20000000000 | bytes 2000000 | tf_op jit(solution)/shard_map/forcing/pallas_call | solution.py:255
  32.0 0.0 all-to-all-done.map_ref
  32.0 3.9 %collective-permute-start = (bf16[512,64]{1,0:T(8,128)(2,1)S(1)}, bf16[512,64]{1,0:T(8,128)(2,1)S(1)}, u32[]{:S(2)}, u32[]{:S(2)}) collective-permute-start(bf16[512,64]{1,0:T(8,128)(2,1)S(1)} %forcing.1.force_ref), channel_id=1, source_target_pairs={{0,1},{1,2},{2,3},{3,4},{4,5},{5,6},{6,7},{7,8},{8,9},{9,10},{10,1... | collective-permute-start | bytes 196616 | tf_op jit(solution)/shard_map/ppermute | solution.py:389
  35.9 0.0 copy-start
  35.9 2.2 %copy-done = bf16[512,64,64]{0,2,1:T(8,128)(2,1)S(1)} copy-done((bf16[512,64,64]{0,2,1:T(8,128)(2,1)S(1)}, bf16[512,64,64]{0,2,1:T(8,128)(2,1)}, u32[]{:S(2)}) %copy-start) | copy-done | bytes 4194328
  38.1 2.1 %impulse_weights.1.wts = bf16[8192,256]{1,0:T(8,128)(2,1)S(1)} custom-call(bf16[4096,512]{1,0:T(8,128)(2,1)S(1)} %bitcast.15), custom_call_target="tpu_custom_call" | custom-call | flops 3000000000 | bytes 8000000 | tf_op jit(solution)/shard_map/impulse_weights/pallas_call | solution.py:298
  40.2 0.0 collective-permute-done.early_ref
  40.2 4.9 %local_stress.1 = bf16[128,512]{1,0:T(8,128)(2,1)S(1)} custom-call(bf16[512,64]{1,0:T(8,128)(2,1)S(1)} %collective-permute-done.early_ref, bf16[512,64]{1,0:T(8,128)(2,1)S(1)} %forcing.1.force_ref, bf16[16,2,256]{2,1,0:T(2,128)(2,1)S(1)} %all-to-all-done.map_ref, bf16[8192,256]{1,0:T(8,128)(2,1)S(1)} %impulse_weights.1.wts), custom_call_target="tpu_custom_call" | custom-call | flops 4000000000 | bytes 5000000 | tf_op jit(solution)/shard_map/local_stress/pallas_call | solution.py:374
  45.1 13.6 %all_to_all.24 = bf16[16,8,512]{2,1,0:T(8,128)(2,1)S(1)} all-to-all(bf16[16,8,512]{2,1,0:T(8,128)(2,1)S(1)} %bitcast.14), channel_id=1, replica_groups=mesh['sea'=2,'tm'=16] {'tm'}, dimensions={0} | all-to-all | bytes 262144 | tf_op jit(solution)/shard_map/all_to_all | solution.py:401
  58.8 0.7 %copy.11 = bf16[8,8192]{1,0:T(8,128)(2,1)} copy(bf16[8,8192]{1,0:T(8,128)(2,1)S(1)} %bitcast.16) | data formatting | bytes 262144
Async XLA Ops:
  1.4 30.6 %all-to-all-start = ((bf16[16,2,256]{2,1,0:T(2,128)(2,1)}), bf16[16,2,256]{2,1,0:T(2,128)(2,1)S(1)}, u32[]{:S(2)}, u32[]{:S(2)}) async-start(bf16[16,2,256]{2,1,0:T(2,128)(2,1)} %tile.9), calls=%async_computation | async-start | bytes 32768 | tf_op jit(solution)/shard_map/all_to_all | solution.py:395
  32.0 8.1 %collective-permute-start = (bf16[512,64]{1,0:T(8,128)(2,1)S(1)}, bf16[512,64]{1,0:T(8,128)(2,1)S(1)}, u32[]{:S(2)}, u32[]{:S(2)}) collective-permute-start(bf16[512,64]{1,0:T(8,128)(2,1)S(1)} %forcing.1.force_ref), channel_id=1, source_target_pairs={{0,1},{1,2},{2,3},{3,4},{4,5},{5,6},{6,7},{7,8},{8,9},{9,10},{10,1... | collective-permute-start | bytes 196616 | tf_op jit(solution)/shard_map/ppermute | solution.py:389
  35.9 2.2 %copy-start = (bf16[512,64,64]{0,2,1:T(8,128)(2,1)S(1)}, bf16[512,64,64]{0,2,1:T(8,128)(2,1)}, u32[]{:S(2)}) copy-start(bf16[512,64,64]{0,2,1:T(8,128)(2,1)} %param.16) | copy-start | bytes 12582916

commit v3 on v2

--- a/solution.py
+++ b/solution.py
@@ -11,7 +11,11 @@
 GIRTH = 500
 LANES = 128
 HALF = 200
-AREA_SCALE = 32767.0
+CUT = 104
+LEAST = 0.2
+CODES = 1023.0
+DECADE = 3.3219280948873626
+BIAS = 2.0 ** -70
 
 
 def pow2_up(x, e, bits):
@@ -20,13 +24,13 @@
     return x
 
 
-def pow2_down(x, bits, top):
+def pow2_down(x, bits):
     e = jnp.zeros(x.shape, I32)
     for b in reversed(range(bits)):
-        big = x >= float(top * 2 ** ((1 << b)))
+        big = x >= 128.0 * BIAS * 2.0 ** (1 << b)
         x = jnp.where(big, x * float(2.0 ** -(1 << b)), x)
         e = e + jnp.where(big, jnp.int32(1 << b), jnp.int32(0))
-    return x, e
+    return x * (1.0 / BIAS), e
 
 
 def shuffled(x, sub):
@@ -41,7 +45,7 @@
     return x
 
 
-def forcing_kernel(st_any, gi_any, cnt_any, pr_any, modes_any, first_ref, second_ref, out_ref,
+def forcing_kernel(st_any, gi_any, cnt_any, pr_any, modes_any, word_ref, out_ref,
                    st_ref, gi_ref, cnt_ref, pr_ref, modes_ref, sems, tab, xs, sc, sr, sp,
                    pc, prow, pp, sel1, sel2, fhv, flv, hiv, lov, wt, rankc):
     steps = st_ref.shape[0]
@@ -52,11 +56,17 @@
     for c in copies:
         c.start()
     for h in range(2):
-        for part, ref in enumerate((first_ref, second_ref)):
-            tab[HALF * part:HALF * (part + 1), LANES * h:LANES * (h + 1)] = ref[HALF * h:HALF * (h + 1), :]
+        lanes = slice(LANES * h, LANES * (h + 1))
+        word = word_ref[HALF * h:HALF * (h + 1), :]
+        first = pow2_up(((word & 127) + 128).astype(F32) * BIAS, ((word >> 7) & 31) + ((word >> 12) & 3) * 32, 7)
+        tab[0:HALF, lanes] = jnp.where((word & (4 << 12)) != 0, -first, first).astype(BF16)
+        upper = word >> 15
+        other = jnp.concatenate([upper[CUT:], jnp.zeros((2 * CUT - HALF, LANES), I32)], axis=0)
+        tab[HALF:, lanes] = pow2_up((upper[:CUT] + 128).astype(F32) * BIAS, other, 7).astype(BF16)
     sub = lax.broadcasted_iota(I32, (8, LANES), 0)
     slot = lax.broadcasted_iota(I32, (LANES, LANES), 1).astype(F32)
     line = lax.broadcasted_iota(I32, (LANES, LANES), 0).astype(F32)
+    line2 = lax.broadcasted_iota(I32, (2 * LANES, LANES), 0).astype(F32)
     copies[0].wait()
     counts = cnt_ref[...].astype(F32)
     n64 = jnp.sum(jnp.where(counts > 64.0, 1.0, 0.0)).astype(I32)
@@ -84,9 +94,9 @@
         xs[here, 0:LANES] = ((panel & 127) + jnp.where(second, LANES, 0)).astype(F32).astype(BF16)
         xs[here, LANES:2 * LANES] = jnp.where(second, hi - HALF, hi).astype(F32).astype(BF16)
         xs[here, 2 * LANES:] = jnp.where(slot < count_col[j], pr_ref[here, :].astype(F32), 0.0).astype(BF16)
-    for j in range(blocks):
-        here = slice(LANES * j, LANES * (j + 1))
-        place = jnp.concatenate([jnp.where(rank_row[i] == line + float(LANES * j), 1.0, 0.0).astype(BF16) for i in range(blocks)], axis=1)
+    for j in range(blocks // 2):
+        here = slice(2 * LANES * j, 2 * LANES * (j + 1))
+        place = jnp.concatenate([jnp.where(rank_row[i] == line2 + float(2 * LANES * j), 1.0, 0.0).astype(BF16) for i in range(blocks)], axis=1)
         y = jnp.dot(place, xs[...], preferred_element_type=F32)
         for i, ref in enumerate((sc, sr, sp)):
             ref[here, :] = y[:, LANES * i:LANES * (i + 1)]
@@ -134,7 +144,9 @@
             for v in range(HALF // 8):
                 hit = want == 8 * v
                 a1 = jnp.where(hit, r[8 * v:8 * v + 8, LANES * j:LANES * (j + 1)], a1)
-                a2 = jnp.where(hit, r[HALF + 8 * v:HALF + 8 * v + 8, LANES * j:LANES * (j + 1)], a2)
+                if 8 * v < CUT:
+                    shared = hit | (want == 8 * v + CUT)
+                    a2 = jnp.where(shared, r[HALF + 8 * v:HALF + 8 * v + 8, LANES * j:LANES * (j + 1)], a2)
             sel1[pl.ds(t0 + j, 1), :] = jnp.sum(a1, axis=0, keepdims=True)
             sel2[pl.ds(t0 + j, 1), :] = jnp.sum(a2, axis=0, keepdims=True)
 
@@ -142,18 +154,19 @@
         here = pl.ds(base, count)
         x1 = sel1[here, :]
         x2 = sel2[here, :]
-        m1, e1 = pow2_down(jnp.abs(x1), 6, 128)
-        m2, e2 = pow2_down(jnp.abs(x2), 6, 128)
-        qi = (m1.astype(I32) - 128) + (e1 << 7) + jnp.where(x1 < 0, 1 << 13, 0) + jnp.where(x2 < 0, 1 << 14, 0) + ((e2 & 1) << 15)
-        f = pp[here, :] * (qi.astype(F32) * (1.0 / AREA_SCALE))
+        m1, e1 = pow2_down(jnp.abs(x1), 7)
+        m2, e2 = pow2_down(x2, 7)
+        upper = jnp.where(prow[here, :] >= float(CUT), e2, m2.astype(I32) - 128)
+        code = (upper << 3) + jnp.where(x1 < 0, 4, 0) + (e1 >> 5)
+        f = pp[here, :] * (LEAST * jnp.exp2(code.astype(F32) * (DECADE / CODES)))
         high = f.astype(BF16).astype(F32)
         fhv[here, :] = high
         flv[here, :] = f - high
-        lov[here, :] = m2 - 128.0
-        hiv[here, :] = e2 >> 1
-
-    sel1[0:group, :] = jnp.full((group, LANES), 128.0, F32)
-    sel2[0:group, :] = jnp.full((group, LANES), 128.0, F32)
+        lov[here, :] = m1 - 128.0
+        hiv[here, :] = e1 & 31
+
+    sel1[0:group, :] = jnp.full((group, LANES), 128.0 * BIAS, F32)
+    sel2[0:group, :] = jnp.full((group, LANES), 128.0 * BIAS, F32)
 
     def lookup(g, carry):
         before = pl.multiple_of(jnp.maximum(g - 1, 0) * group, group)
@@ -213,16 +226,17 @@
 
     copies[4].wait()
     ordered = []
-    for j in range(blocks):
-        here = slice(LANES * j, LANES * (j + 1))
-        acc = jnp.zeros((2 * LANES, modes), F32)
+    many = 2 * LANES
+    for j in range(steps // many):
+        here = slice(many * j, many * (j + 1))
+        acc = jnp.zeros((2 * many, modes), F32)
         for h in range(high_parts // 2):
             w = jnp.concatenate([wt[2 * h, here, :], wt[2 * h + 1, here, :]], axis=1)
             wh = w.astype(BF16)
             wl = (w - wh.astype(F32)).astype(BF16)
             acc = acc + lax.dot_general(jnp.concatenate([wh, wl], axis=0), modes_ref[:, 256 * h:256 * h + 256],
                                         (((1,), (1,)), ((), ())), preferred_element_type=F32)
-        ordered.append((acc[:LANES] + acc[LANES:]).astype(BF16))
+        ordered.append((acc[:many] + acc[many:]).astype(BF16))
     ordered = jnp.concatenate(ordered, axis=0)
     for j in range(blocks):
         here = slice(LANES * j, LANES * (j + 1))
@@ -236,31 +250,26 @@
 
 def encoded(panel_area, panel_patch):
     pad = 2 * HALF * LANES - panel_area.shape[0]
-    q = (jnp.pad(panel_area, (0, pad)) * AREA_SCALE + 0.5).astype(I32)
-    patch = jnp.pad(panel_patch, (0, pad))
-    first = pow2_up(((q & 127) + 128).astype(F32), (q >> 7) & 63, 6)
-    first = jnp.where(((q >> 13) & 1) == 1, -first, first).astype(BF16)
-    second = pow2_up(((patch & 127) + 128).astype(F32), (patch >> 7) * 2 + (q >> 15), 6)
-    second = jnp.where(((q >> 14) & 1) == 1, -second, second).astype(BF16)
-    return first.reshape(2 * HALF, LANES), second.reshape(2 * HALF, LANES)
+    code = jnp.clip((jnp.log2(panel_area * (1.0 / LEAST)) * (CODES / DECADE) + 0.5).astype(I32), 0, int(CODES))
+    return jnp.pad(panel_patch + (code << 12), (0, pad)).reshape(2 * HALF, LANES)
 
 
 def forcing(wet_station, wet_girth, wet_count, pressure, panel_area, panel_patch, patch_modes):
     steps = wet_station.shape[0]
     patches, modes = patch_modes.shape
-    first, second = encoded(panel_area, panel_patch)
+    words = encoded(panel_area, panel_patch)
     far = (wet_station, wet_girth, wet_count.reshape(steps // LANES, LANES), pressure, patch_modes.T)
     far = tuple(pltpu.with_memory_space_constraint(x, pltpu.HBM) for x in far)
     table = lambda n, t: pltpu.VMEM((n, LANES), t)
     return pl.pallas_call(
         forcing_kernel,
         out_shape=jax.ShapeDtypeStruct((steps, modes), BF16),
-        in_specs=[pl.BlockSpec(memory_space=pltpu.HBM)] * 5 + [pl.BlockSpec(memory_space=pltpu.VMEM)] * 2,
+        in_specs=[pl.BlockSpec(memory_space=pltpu.HBM)] * 5 + [pl.BlockSpec(memory_space=pltpu.VMEM)],
         out_specs=pl.BlockSpec(memory_space=pltpu.VMEM),
         scratch_shapes=[
             *[pltpu.VMEM(x.shape, x.dtype) for x in far],
             pltpu.SemaphoreType.DMA((5,)),
-            pltpu.VMEM((2 * HALF, 256), BF16),
+            pltpu.VMEM((HALF + CUT, 256), BF16),
             pltpu.VMEM((steps, 3 * LANES), BF16),
             *[table(steps + LANES, F32)] * 3,
             *[table(steps, F32)] * 7,
@@ -271,14 +280,18 @@
         compiler_params=pltpu.CompilerParams(vmem_limit_bytes=24 * 1024 * 1024),
         cost_estimate=pl.CostEstimate(flops=2 * 10 ** 10, bytes_accessed=2 * 10 ** 6, transcendentals=0),
         name="forcing",
-    )(*far, first, second)
-
-
-def weights_kernel(imp_ref, out_ref):
+    )(*far, words)
+
+
+def weights_kernel(imp_any, out_ref, imp_ref, sems):
     modes = out_ref.shape[1] // 4
     quarter = imp_ref.shape[1] // 4
     row = lax.broadcasted_iota(I32, (2 * quarter, 2 * quarter), 0)
     col = lax.broadcasted_iota(I32, (2 * quarter, 2 * quarter), 1)
+    chunk = imp_ref.shape[0] // 4
+    copies = [pltpu.make_async_copy(imp_any.at[pl.ds(chunk * c, chunk), :], imp_ref.at[pl.ds(chunk * c, chunk), :], sems.at[c]) for c in range(4)]
+    for c in copies:
+        c.start()
     order = jnp.where(((row >> 3) & 1) * quarter + (row >> 4) * 8 + (row & 7) == col, 1.0, 0.0).astype(BF16)
 
     def turn(i, carry):
@@ -289,7 +302,9 @@
             out_ref[pl.ds(pl.multiple_of(v * (8 * modes) + 16 * i, 16), 16), :] = y[16 * v:16 * v + 16]
         return carry
 
-    lax.fori_loop(0, modes // 2, turn, 0, unroll=8)
+    for c in range(4):
+        copies[c].wait()
+        lax.fori_loop(modes // 8 * c, modes // 8 * (c + 1), turn, 0, unroll=True)
 
 
 def impulse_weights(impulse):
@@ -298,12 +313,13 @@
     return pl.pallas_call(
         weights_kernel,
         out_shape=jax.ShapeDtypeStruct((lags // 4 * modes, 4 * modes), BF16),
-        in_specs=[pl.BlockSpec(memory_space=pltpu.VMEM)],
+        in_specs=[pl.BlockSpec(memory_space=pltpu.HBM)],
         out_specs=pl.BlockSpec(memory_space=pltpu.VMEM),
-        compiler_params=pltpu.CompilerParams(vmem_limit_bytes=8 * 1024 * 1024),
+        scratch_shapes=[pltpu.VMEM(flat.shape, BF16), pltpu.SemaphoreType.DMA((4,))],
+        compiler_params=pltpu.CompilerParams(vmem_limit_bytes=12 * 1024 * 1024),
         cost_estimate=pl.CostEstimate(flops=3 * 10 ** 9, bytes_accessed=8 * 10 ** 6, transcendentals=0),
         name="impulse_weights",
-    )(flat)
+    )(pltpu.with_memory_space_constraint(flat, pltpu.HBM))
 
 
 def products(seq, wts, pair, x8, shifts, acc):
@@ -321,8 +337,9 @@
     col = lax.broadcasted_iota(I32, (8 * modes, 8 * modes), 1)
     spread = jnp.where((row & (modes - 1)) * 8 + row // modes == col, 1.0, 0.0).astype(BF16)
     last = jnp.zeros((8, 8 * modes), F32)
-    for k in range(count // LANES):
-        here = slice(LANES * k, LANES * (k + 1))
+    big = 4 * LANES
+    for k in range(count // big):
+        here = slice(big * k, big * (k + 1))
         y = jnp.dot(x8[here, :], spread, preferred_element_type=F32)
         shifts[here, 0:8 * modes] = y.astype(BF16)
         shifts[here, 8 * modes:] = jnp.concatenate([last, y[:-8]], axis=0).astype(BF16)
@@ -349,13 +366,7 @@
     lane = lax.broadcasted_iota(I32, (steps, 2 * modes), 1) < modes
     s = jnp.where(lane, y(0), y(1)) + jnp.where(lane, y(2), y(3))
     response = (s[:, :modes] + s[:, modes:]).astype(BF16)
-    flat = map_ref[...].reshape(-1, map_ref.shape[2])
-    lines, folds = flat.shape[0], flat.shape[1] // modes
-    parts = jnp.concatenate([flat[:, modes * b:modes * (b + 1)] for b in range(folds)], axis=0)
-    row = lax.broadcasted_iota(I32, (lines * folds, lines * folds), 0)
-    col = lax.broadcasted_iota(I32, (lines * folds, lines * folds), 1)
-    order = jnp.where((row & (folds - 1)) * lines + row // folds == col, 1.0, 0.0).astype(BF16)
-    hot_map = jnp.dot(order, parts, preferred_element_type=F32).astype(BF16)
+    hot_map = map_ref[...].reshape(-1, 2 * modes)[:, :modes]
     out_ref[...] = lax.dot_general(hot_map, response, (((1,), (1,)), ((), ())), preferred_element_type=F32).astype(BF16)
 
 
@@ -370,7 +381,7 @@
 def local_stress(early, force, whole_map, weights):
     steps, modes = force.shape
     quarter = weights.shape[0] // modes
-    hot = whole_map.size // modes
+    hot = whole_map.shape[0] * whole_map.shape[1]
     return pl.pallas_call(
         stress_kernel,
         out_shape=jax.ShapeDtypeStruct((hot, steps), BF16),
@@ -391,7 +402,7 @@
 
 def body(wet_station, wet_girth, wet_count, pressure, panel_area, panel_patch, patch_modes, impulse, stress_map):
     steps = wet_station.shape[0]
-    own_map = jnp.tile(stress_map.T.reshape(1, -1, 256), (lax.axis_size("tm"), 1, 1))
+    own_map = jnp.tile(stress_map.T[None], (lax.axis_size("tm"), 1, 2))
     whole_map = lax.all_to_all(own_map, "tm", 0, 0, tiled=True)
     force = forcing(wet_station, wet_girth, wet_count, pressure, panel_area, panel_patch, patch_modes)
     force, whole_map = lax.optimization_barrier((force, whole_map))

time: 59.7 us -> 56.5 us (0.946)
  local copies, waits for them, and re-layouts: 4.22 us -> 2.06 us
  Pallas kernels: 28.7 us -> 27.9 us
  blocking collectives: 13.6 us -> 14.3 us
    unnamed x3 -> x1, local copies, waits for them, and re-layouts: 2.84 us -> 0.66 us
    pallas_call x1, Pallas kernels: 21.7 us -> 19.8 us  [forcing(): pl.pallas_call(forcing_kernel, out_shape=jax.ShapeDtypeStruct((steps, mod...]
    reshape x1 -> x0, other arithmetic: 1.53 us -> none  [encoded(): return (first.reshape(2 * HALF, LANES), second.reshape(2 * HALF, LANES))]
    add x0 -> x1, other arithmetic: none -> 1.12 us  [encoded(): panel_patch + (code << 12)]
    pallas_call x1, Pallas kernels: 2.05 us -> 3.15 us  [impulse_weights(): pl.pallas_call(weights_kernel, out_shape=jax.ShapeDtypeStruct((lags // 4...]
    all_to_all x1, blocking collectives: 13.6 us -> 14.3 us  [body(): return lax.all_to_all(part, 'tm', 0, 1, tiled=True)]
    another operation x2 -> x3, local copies, waits for them, and re-layouts: 1.38 us -> 1.39 us  [body(): own_map = jnp.tile(stress_map.T[None], (lax.axis_size('tm'), 1, 2))]
  transfers between devices with their start and end apart: 2 -> 2, of which waited for: 0 -> 0; matrix products, arithmetic and copies ran while one was open for 3% -> 2% of each run, Pallas kernels for 40% -> 40%
where the time goes in v3:
time: 56.5 us; the launch traced here: 56.7 us
  Pallas kernels  27.9 us (49%)
  blocking collectives  14.3 us (25%)
  starting transfers between devices  11.2 us (20%)
  local copies, waits for them, and re-layouts  2.06 us (4%)
  other arithmetic  1.12 us (2%)
    pallas_call x1, Pallas kernels, forcing(): pl.pallas_call(forcing_kernel, out_shape=jax.ShapeDtypeStruct((steps, mod...  19.8 us
    all_to_all x1, blocking collectives, body(): return lax.all_to_all(part, 'tm', 0, 1, tiled=True)  14.3 us
    all_to_all x1, starting transfers between devices, body(): whole_map = lax.all_to_all(own_map, 'tm', 0, 0, tiled=True)  7.36 us
    pallas_call x1, Pallas kernels, local_stress(): pl.pallas_call(stress_kernel, out_shape=jax.ShapeDtypeStruct((hot, steps)...  4.95 us
    ppermute x1, starting transfers between devices, shifted(): lax.ppermute(value, axis, [(source, source + steps) for source in range(l...  3.87 us
    pallas_call x1, Pallas kernels, impulse_weights(): pl.pallas_call(weights_kernel, out_shape=jax.ShapeDtypeStruct((lags // 4...  3.15 us
    another operation x3, local copies, waits for them, and re-layouts, body(): own_map = jnp.tile(stress_map.T[None], (lax.axis_size('tm'), 1, 2))  1.39 us
  transfers between devices with their start and end apart: 2, of which 0 were waited for; matrix products, arithmetic and copies ran while one was open for 2% of the time, Pallas kernels for 40%

profile of v3, /device:TPU:0, one launch (start us, length us, event | category | flops | bytes accessed | tf_op | source)
XLA Modules:
  0.0 56.7 jit_solution(4390978083268259830)
XLA Ops:
  0.0 0.7 %tile.10 = bf16[8,2,64]{2,1,0:T(2,128)(2,1)S(1)} broadcast(bf16[8,64]{1,0:T(8,128)(2,1)} %bitcast.14), dimensions={0,2} | broadcast | bytes 3072 | tf_op jit(solution)/shard_map/tile | solution.py:405
  0.7 0.1 tile.11
  0.8 0.6 %tile.12 = bf16[16,8,128]{2,1,0:T(8,128)(2,1)} broadcast(bf16[8,128]{1,0:T(8,128)(2,1)S(1)} %tile.11), dimensions={1,2} | broadcast | bytes 34816 | tf_op jit(solution)/shard_map/tile | solution.py:405
  1.4 7.4 %all-to-all-start = ((bf16[16,8,128]{2,1,0:T(8,128)(2,1)}), bf16[16,8,128]{2,1,0:T(8,128)(2,1)S(1)}, u32[]{:S(2)}, u32[]{:S(2)}) async-start(bf16[16,8,128]{2,1,0:T(8,128)(2,1)} %tile.12), calls=%async_computation | async-start | bytes 65536 | tf_op jit(solution)/shard_map/all_to_all | solution.py:406
  8.8 1.1 %shift-left_add_fusion = s32[50000]{0:T(1024)S(1)} fusion(s32[50000]{0:T(1024)} %param.14, f32[50000]{0:T(1024)} %param.13), kind=kLoop, calls=%fused_computation.1 | loop fusion | flops 350000 | bytes 600000 | tf_op jit(solution)/shard_map/add | solution.py:254
  9.9 19.8 %forcing.1.force_ref = bf16[512,64]{1,0:T(8,128)(2,1)S(1)} custom-call(s32[512,128]{1,0:T(8,128)} %st_any.1, s32[512,128]{1,0:T(8,128)} %gi_any.1, s32[4,128]{1,0:T(4,128)} %bitcast.17, bf16[512,128]{1,0:T(8,128)(2,1)} %pr_any.1, bf16[64,3072]{1,0:T(8,128)(2,1)} %bitcast.16, s32[400,128]{1,0:T(8,128)S(1)} %pad_bitcast_fusion.word_ref), custom_call_target="tpu_custom_call" | custom-call | flops 20000000000 | bytes 2000000 | tf_op jit(solution)/shard_map/forcing/pallas_call | solution.py:264
  29.7 0.0 all-to-all-done.map_ref
  29.7 3.9 %collective-permute-start = (bf16[512,64]{1,0:T(8,128)(2,1)S(1)}, bf16[512,64]{1,0:T(8,128)(2,1)S(1)}, u32[]{:S(2)}, u32[]{:S(2)}) collective-permute-start(bf16[512,64]{1,0:T(8,128)(2,1)S(1)} %forcing.1.force_ref), channel_id=1, source_target_pairs={{0,1},{1,2},{2,3},{3,4},{4,5},{5,6},{6,7},{7,8},{8,9},{9,10},{10,1... | collective-permute-start | bytes 196616 | tf_op jit(solution)/shard_map/ppermute | solution.py:400
  33.6 3.2 %impulse_weights.1.wts = bf16[8192,256]{1,0:T(8,128)(2,1)S(1)} custom-call(bf16[4096,512]{1,0:T(8,128)(2,1)} %bitcast.15), custom_call_target="tpu_custom_call" | custom-call | flops 3000000000 | bytes 8000000 | tf_op jit(solution)/shard_map/impulse_weights/pallas_call | solution.py:313
  36.7 0.0 collective-permute-done.early_ref
  36.8 4.9 %local_stress.1 = bf16[128,512]{1,0:T(8,128)(2,1)S(1)} custom-call(bf16[512,64]{1,0:T(8,128)(2,1)S(1)} %collective-permute-done.early_ref, bf16[512,64]{1,0:T(8,128)(2,1)S(1)} %forcing.1.force_ref, bf16[16,8,128]{2,1,0:T(8,128)(2,1)S(1)} %all-to-all-done.map_ref, bf16[8192,256]{1,0:T(8,128)(2,1)S(1)} %impulse_weights.1.wts), custom_call_target="tpu_custom_call" | custom-call | flops 4000000000 | bytes 5000000 | tf_op jit(solution)/shard_map/local_stress/pallas_call | solution.py:385
  41.7 14.3 %all_to_all.24 = bf16[16,8,512]{2,1,0:T(8,128)(2,1)S(1)} all-to-all(bf16[16,8,512]{2,1,0:T(8,128)(2,1)S(1)} %bitcast.12), channel_id=1, replica_groups=mesh['sea'=2,'tm'=16] {'tm'}, dimensions={0} | all-to-all | bytes 262144 | tf_op jit(solution)/shard_map/all_to_all | solution.py:412
  56.1 0.7 %copy.11 = bf16[8,8192]{1,0:T(8,128)(2,1)} copy(bf16[8,8192]{1,0:T(8,128)(2,1)S(1)} %bitcast.13) | data formatting | bytes 262144
  (1 shorter events, 0.0 us)
Async XLA Ops:
  1.4 28.3 %all-to-all-start = ((bf16[16,8,128]{2,1,0:T(8,128)(2,1)}), bf16[16,8,128]{2,1,0:T(8,128)(2,1)S(1)}, u32[]{:S(2)}, u32[]{:S(2)}) async-start(bf16[16,8,128]{2,1,0:T(8,128)(2,1)} %tile.12), calls=%async_computation | async-start | bytes 65536 | tf_op jit(solution)/shard_map/all_to_all | solution.py:406
  29.7 7.0 %collective-permute-start = (bf16[512,64]{1,0:T(8,128)(2,1)S(1)}, bf16[512,64]{1,0:T(8,128)(2,1)S(1)}, u32[]{:S(2)}, u32[]{:S(2)}) collective-permute-start(bf16[512,64]{1,0:T(8,128)(2,1)S(1)} %forcing.1.force_ref), channel_id=1, source_target_pairs={{0,1},{1,2},{2,3},{3,4},{4,5},{5,6},{6,7},{7,8},{8,9},{9,10},{10,1... | collective-permute-start | bytes 196616 | tf_op jit(solution)/shard_map/ppermute | solution.py:400

commit v4 on v3

--- a/solution.py
+++ b/solution.py
@@ -107,6 +107,10 @@
     n_full = (n64 + (group - 1)) // group
     base2 = n_full * group
     n_half = (jnp.maximum(n32 - base2, 0) + (2 * group - 1)) // (2 * group)
+    left = jnp.maximum(steps - base2 - n_half * 2 * group, 0) // group
+    n_full = n_full + jnp.where(left % 4 == 1, 1, 0)
+    n_half = n_half + jnp.where(left % 4 == 2, 1, 0)
+    base2 = n_full * group
     base4 = base2 + n_half * 2 * group
     n_quarter = (jnp.maximum(steps - base4, 0) + (4 * group - 1)) // (4 * group)
     n_all = n_full + n_half + n_quarter
@@ -177,7 +181,12 @@
                 decode(pl.multiple_of(before + 8 * (p // 4), 8), 8)
         return carry
 
-    lax.fori_loop(0, n_all, lookup, 0)
+    def lookup_two(i, carry):
+        lookup(2 * i, carry)
+        return lookup(2 * i + 1, carry)
+
+    lax.fori_loop(0, n_all // 2, lookup_two, 0)
+    lax.fori_loop(n_all // 2 * 2, n_all, lookup, 0)
     decode(pl.multiple_of((n_all - 1) * group, group), group)
 
 
@@ -222,7 +231,15 @@
                         for i, x in enumerate(shuffled([y[8 * hb:8 * hb + 8] for y in sums[c]], sub)):
                             wt[8 * hb + i, spot, :] = x
             return carry
-        lax.fori_loop(0, n, scatter, 0)
+        if pack < 4:
+            def scatter_two(i, carry):
+                scatter(2 * i, carry)
+                return scatter(2 * i + 1, carry)
+
+            lax.fori_loop(0, n // 2, scatter_two, 0)
+            lax.fori_loop(n // 2 * 2, n, scatter, 0)
+        else:
+            lax.fori_loop(0, n, scatter, 0)
 
     copies[4].wait()
     ordered = []
@@ -402,7 +419,8 @@
 
 def body(wet_station, wet_girth, wet_count, pressure, panel_area, panel_patch, patch_modes, impulse, stress_map):
     steps = wet_station.shape[0]
-    own_map = jnp.tile(stress_map.T[None], (lax.axis_size("tm"), 1, 2))
+    hot, modes = stress_map.shape[1], stress_map.shape[0]
+    own_map = jnp.broadcast_to(jnp.pad(stress_map.T, ((0, 0), (0, modes)))[None], (lax.axis_size("tm"), hot, 2 * modes))
     whole_map = lax.all_to_all(own_map, "tm", 0, 0, tiled=True)
     force = forcing(wet_station, wet_girth, wet_count, pressure, panel_area, panel_patch, patch_modes)
     force, whole_map = lax.optimization_barrier((force, whole_map))

time: 56.5 us -> 54.8 us (0.970); the launches traced: 56.7 us -> 54.1 us
  starting transfers between devices: 11.2 us -> 9.86 us
  blocking collectives: 14.3 us -> 13.4 us
    another operation x3 -> x0, local copies, waits for them, and re-layouts: 1.39 us -> none  [body(): own_map = jnp.tile(stress_map.T[None], (lax.axis_size('tm'), 1, 2))]
    ppermute x1, starting transfers between devices: 3.87 us -> 2.5 us  [shifted(): lax.ppermute(value, axis, [(source, source + steps) for source in range(l...]
    all_to_all x1, blocking collectives: 14.3 us -> 13.4 us  [body(): return lax.all_to_all(part, 'tm', 0, 1, tiled=True)]
    pad x0 -> x1, local copies, waits for them, and re-layouts: none -> 0.69 us  [body(): jnp.pad(stress_map.T, ((0, 0), (0, modes)))[None]]
    broadcast_in_dim x0 -> x1, local copies, waits for them, and re-layouts: none -> 0.62 us  [body(): jnp.broadcast_to(jnp.pad(stress_map.T, ((0, 0), (0, modes)))[None], (lax....]
  transfers between devices with their start and end apart: 2 -> 2, of which waited for: 0 -> 0; matrix products, arithmetic and copies ran while one was open for 2% -> 2% of each run, Pallas kernels for 40% -> 42%
where the time goes in v4:
time: 54.8 us; the launch traced here: 54.1 us
  Pallas kernels  27.6 us (50%)
  blocking collectives  13.4 us (24%)
  starting transfers between devices  9.86 us (18%)
  local copies, waits for them, and re-layouts  1.98 us (4%)
  other arithmetic  1.12 us (2%)
    pallas_call x1, Pallas kernels, forcing(): pl.pallas_call(forcing_kernel, out_shape=jax.ShapeDtypeStruct((steps, mod...  19.5 us
    all_to_all x1, blocking collectives, body(): return lax.all_to_all(part, 'tm', 0, 1, tiled=True)  13.4 us
    all_to_all x1, starting transfers between devices, body(): whole_map = lax.all_to_all(own_map, 'tm', 0, 0, tiled=True)  7.36 us
    pallas_call x1, Pallas kernels, local_stress(): pl.pallas_call(stress_kernel, out_shape=jax.ShapeDtypeStruct((hot, steps)...  4.95 us
    pallas_call x1, Pallas kernels, impulse_weights(): pl.pallas_call(weights_kernel, out_shape=jax.ShapeDtypeStruct((lags // 4...  3.15 us
    ppermute x1, starting transfers between devices, shifted(): lax.ppermute(value, axis, [(source, source + steps) for source in range(l...  2.5 us
    add x1, other arithmetic, encoded(): panel_patch + (code << 12)  1.12 us
  transfers between devices with their start and end apart: 2, of which 0 were waited for; matrix products, arithmetic and copies ran while one was open for 2% of the time, Pallas kernels for 42%

profile of v4, /device:TPU:0, one launch (start us, length us, event | category | flops | bytes accessed | tf_op | source)
XLA Modules:
  0.0 54.1 jit_solution(7688487857536288798)
XLA Ops:
  0.0 0.7 %pad.9 = bf16[8,128]{1,0:T(8,128)(2,1)S(1)} pad(bf16[8,64]{1,0:T(8,128)(2,1)} %bitcast.14, bf16[]{:T(256)} %constant.15.clone.1), padding=0_0x0_64 | pad | bytes 3074 | tf_op jit(solution)/shard_map/jit(_pad)/pad | solution.py:423
  0.7 0.6 %broadcast_in_dim.2 = bf16[16,8,128]{2,1,0:T(8,128)(2,1)} broadcast(bf16[8,128]{1,0:T(8,128)(2,1)S(1)} %pad.9), dimensions={1,2} | broadcast | bytes 34816 | tf_op jit(solution)/shard_map/broadcast_in_dim | solution.py:423
  1.3 7.4 %all-to-all-start = ((bf16[16,8,128]{2,1,0:T(8,128)(2,1)}), bf16[16,8,128]{2,1,0:T(8,128)(2,1)S(1)}, u32[]{:S(2)}, u32[]{:S(2)}) async-start(bf16[16,8,128]{2,1,0:T(8,128)(2,1)} %broadcast_in_dim.2), calls=%async_computation | async-start | bytes 65536 | tf_op jit(solution)/shard_map/all_to_all | solution.py:424
  8.7 1.1 %shift-left_add_fusion = s32[50000]{0:T(1024)S(1)} fusion(s32[50000]{0:T(1024)} %param.14, f32[50000]{0:T(1024)} %param.13), kind=kLoop, calls=%fused_computation.1 | loop fusion | flops 350000 | bytes 600000 | tf_op jit(solution)/shard_map/add | solution.py:271
  9.8 19.5 %forcing.1.force_ref = bf16[512,64]{1,0:T(8,128)(2,1)S(1)} custom-call(s32[512,128]{1,0:T(8,128)} %st_any.1, s32[512,128]{1,0:T(8,128)} %gi_any.1, s32[4,128]{1,0:T(4,128)} %bitcast.17, bf16[512,128]{1,0:T(8,128)(2,1)} %pr_any.1, bf16[64,3072]{1,0:T(8,128)(2,1)} %bitcast.16, s32[400,128]{1,0:T(8,128)S(1)} %pad_bitcast_fusion.word_ref), custom_call_target="tpu_custom_call" | custom-call | flops 20000000000 | bytes 2000000 | tf_op jit(solution)/shard_map/forcing/pallas_call | solution.py:281
  29.3 0.0 all-to-all-done.map_ref
  29.3 2.5 %collective-permute-start = (bf16[512,64]{1,0:T(8,128)(2,1)S(1)}, bf16[512,64]{1,0:T(8,128)(2,1)S(1)}, u32[]{:S(2)}, u32[]{:S(2)}) collective-permute-start(bf16[512,64]{1,0:T(8,128)(2,1)S(1)} %forcing.1.force_ref), channel_id=1, source_target_pairs={{0,1},{1,2},{2,3},{3,4},{4,5},{5,6},{6,7},{7,8},{8,9},{9,10},{10,1... | collective-permute-start | bytes 196616 | tf_op jit(solution)/shard_map/ppermute | solution.py:417
  31.9 3.2 %impulse_weights.1.wts = bf16[8192,256]{1,0:T(8,128)(2,1)S(1)} custom-call(bf16[4096,512]{1,0:T(8,128)(2,1)} %bitcast.15), custom_call_target="tpu_custom_call" | custom-call | flops 3000000000 | bytes 8000000 | tf_op jit(solution)/shard_map/impulse_weights/pallas_call | solution.py:330
  35.0 0.0 collective-permute-done.early_ref
  35.0 4.9 %local_stress.1 = bf16[128,512]{1,0:T(8,128)(2,1)S(1)} custom-call(bf16[512,64]{1,0:T(8,128)(2,1)S(1)} %collective-permute-done.early_ref, bf16[512,64]{1,0:T(8,128)(2,1)S(1)} %forcing.1.force_ref, bf16[16,8,128]{2,1,0:T(8,128)(2,1)S(1)} %all-to-all-done.map_ref, bf16[8192,256]{1,0:T(8,128)(2,1)S(1)} %impulse_weights.1.wts), custom_call_target="tpu_custom_call" | custom-call | flops 4000000000 | bytes 5000000 | tf_op jit(solution)/shard_map/local_stress/pallas_call | solution.py:402
  40.0 13.4 %all_to_all.24 = bf16[16,8,512]{2,1,0:T(8,128)(2,1)S(1)} all-to-all(bf16[16,8,512]{2,1,0:T(8,128)(2,1)S(1)} %bitcast.12), channel_id=1, replica_groups=mesh['sea'=2,'tm'=16] {'tm'}, dimensions={0} | all-to-all | bytes 262144 | tf_op jit(solution)/shard_map/all_to_all | solution.py:430
  53.4 0.7 %copy.11 = bf16[8,8192]{1,0:T(8,128)(2,1)} copy(bf16[8,8192]{1,0:T(8,128)(2,1)S(1)} %bitcast.13) | data formatting | bytes 262144
  (1 shorter events, 0.0 us)
Async XLA Ops:
  1.3 28.0 %all-to-all-start = ((bf16[16,8,128]{2,1,0:T(8,128)(2,1)}), bf16[16,8,128]{2,1,0:T(8,128)(2,1)S(1)}, u32[]{:S(2)}, u32[]{:S(2)}) async-start(bf16[16,8,128]{2,1,0:T(8,128)(2,1)} %broadcast_in_dim.2), calls=%async_computation | async-start | bytes 65536 | tf_op jit(solution)/shard_map/all_to_all | solution.py:424
  29.3 5.7 %collective-permute-start = (bf16[512,64]{1,0:T(8,128)(2,1)S(1)}, bf16[512,64]{1,0:T(8,128)(2,1)S(1)}, u32[]{:S(2)}, u32[]{:S(2)}) collective-permute-start(bf16[512,64]{1,0:T(8,128)(2,1)S(1)} %forcing.1.force_ref), channel_id=1, source_target_pairs={{0,1},{1,2},{2,3},{3,4},{4,5},{5,6},{6,7},{7,8},{8,9},{9,10},{10,1... | collective-permute-start | bytes 196616 | tf_op jit(solution)/shard_map/ppermute | solution.py:417

commit v5 on v4

--- a/solution.py
+++ b/solution.py
@@ -305,8 +305,8 @@
     quarter = imp_ref.shape[1] // 4
     row = lax.broadcasted_iota(I32, (2 * quarter, 2 * quarter), 0)
     col = lax.broadcasted_iota(I32, (2 * quarter, 2 * quarter), 1)
-    chunk = imp_ref.shape[0] // 4
-    copies = [pltpu.make_async_copy(imp_any.at[pl.ds(chunk * c, chunk), :], imp_ref.at[pl.ds(chunk * c, chunk), :], sems.at[c]) for c in range(4)]
+    chunk = imp_ref.shape[0] // 2
+    copies = [pltpu.make_async_copy(imp_any.at[pl.ds(chunk * c, chunk), :], imp_ref.at[pl.ds(chunk * c, chunk), :], sems.at[c]) for c in range(2)]
     for c in copies:
         c.start()
     order = jnp.where(((row >> 3) & 1) * quarter + (row >> 4) * 8 + (row & 7) == col, 1.0, 0.0).astype(BF16)
@@ -319,9 +319,9 @@
             out_ref[pl.ds(pl.multiple_of(v * (8 * modes) + 16 * i, 16), 16), :] = y[16 * v:16 * v + 16]
         return carry
 
-    for c in range(4):
+    for c in range(2):
         copies[c].wait()
-        lax.fori_loop(modes // 8 * c, modes // 8 * (c + 1), turn, 0, unroll=True)
+        lax.fori_loop(modes // 4 * c, modes // 4 * (c + 1), turn, 0, unroll=True)
 
 
 def impulse_weights(impulse):
@@ -332,7 +332,7 @@
         out_shape=jax.ShapeDtypeStruct((lags // 4 * modes, 4 * modes), BF16),
         in_specs=[pl.BlockSpec(memory_space=pltpu.HBM)],
         out_specs=pl.BlockSpec(memory_space=pltpu.VMEM),
-        scratch_shapes=[pltpu.VMEM(flat.shape, BF16), pltpu.SemaphoreType.DMA((4,))],
+        scratch_shapes=[pltpu.VMEM(flat.shape, BF16), pltpu.SemaphoreType.DMA((2,))],
         compiler_params=pltpu.CompilerParams(vmem_limit_bytes=12 * 1024 * 1024),
         cost_estimate=pl.CostEstimate(flops=3 * 10 ** 9, bytes_accessed=8 * 10 ** 6, transcendentals=0),
         name="impulse_weights",
@@ -354,7 +354,7 @@
     col = lax.broadcasted_iota(I32, (8 * modes, 8 * modes), 1)
     spread = jnp.where((row & (modes - 1)) * 8 + row // modes == col, 1.0, 0.0).astype(BF16)
     last = jnp.zeros((8, 8 * modes), F32)
-    big = 4 * LANES
+    big = count
     for k in range(count // big):
         here = slice(big * k, big * (k + 1))
         y = jnp.dot(x8[here, :], spread, preferred_element_type=F32)

time: 54.8 us -> 56.1 us (1.024)
  blocking collectives: 13.4 us -> 14.4 us
    all_to_all x1, blocking collectives: 13.4 us -> 14.4 us  [body(): return lax.all_to_all(part, 'tm', 0, 1, tiled=True)]
    pallas_call x1, Pallas kernels: 4.95 us -> 5.8 us  [local_stress(): pl.pallas_call(stress_kernel, out_shape=jax.ShapeDtypeStruct((hot, steps)...]
  transfers between devices with their start and end apart: 2 -> 2, of which waited for: 0 -> 0; matrix products, arithmetic and copies ran while one was open for 2% -> 2% of each run, Pallas kernels for 42% -> 40%
where the time goes in v5:
time: 56.1 us; the launch traced here: 55.8 us
  Pallas kernels  28 us (50%)
  blocking collectives  14.4 us (26%)
  starting transfers between devices  10.3 us (18%)
  local copies, waits for them, and re-layouts  1.98 us (4%)
  other arithmetic  1.12 us (2%)
    pallas_call x1, Pallas kernels, forcing(): pl.pallas_call(forcing_kernel, out_shape=jax.ShapeDtypeStruct((steps, mod...  19 us
    all_to_all x1, blocking collectives, body(): return lax.all_to_all(part, 'tm', 0, 1, tiled=True)  14.4 us
    all_to_all x1, starting transfers between devices, body(): whole_map = lax.all_to_all(own_map, 'tm', 0, 0, tiled=True)  7.36 us
    pallas_call x1, Pallas kernels, local_stress(): pl.pallas_call(stress_kernel, out_shape=jax.ShapeDtypeStruct((hot, steps)...  5.8 us
    pallas_call x1, Pallas kernels, impulse_weights(): pl.pallas_call(weights_kernel, out_shape=jax.ShapeDtypeStruct((lags // 4...  3.1 us
    ppermute x1, starting transfers between devices, shifted(): lax.ppermute(value, axis, [(source, source + steps) for source in range(l...  2.96 us
  transfers between devices with their start and end apart: 2, of which 0 were waited for; matrix products, arithmetic and copies ran while one was open for 2% of the time, Pallas kernels for 40%

profile of v5, /device:TPU:0, one launch (start us, length us, event | category | flops | bytes accessed | tf_op | source)
XLA Modules:
  0.0 55.8 jit_solution(14872106218450610724)
XLA Ops:
  0.0 0.7 %pad.9 = bf16[8,128]{1,0:T(8,128)(2,1)S(1)} pad(bf16[8,64]{1,0:T(8,128)(2,1)} %bitcast.14, bf16[]{:T(256)} %constant.15.clone.1), padding=0_0x0_64 | pad | bytes 3074 | tf_op jit(solution)/shard_map/jit(_pad)/pad | solution.py:423
  0.7 0.6 %broadcast_in_dim.2 = bf16[16,8,128]{2,1,0:T(8,128)(2,1)} broadcast(bf16[8,128]{1,0:T(8,128)(2,1)S(1)} %pad.9), dimensions={1,2} | broadcast | bytes 34816 | tf_op jit(solution)/shard_map/broadcast_in_dim | solution.py:423
  1.3 7.4 %all-to-all-start = ((bf16[16,8,128]{2,1,0:T(8,128)(2,1)}), bf16[16,8,128]{2,1,0:T(8,128)(2,1)S(1)}, u32[]{:S(2)}, u32[]{:S(2)}) async-start(bf16[16,8,128]{2,1,0:T(8,128)(2,1)} %broadcast_in_dim.2), calls=%async_computation | async-start | bytes 65536 | tf_op jit(solution)/shard_map/all_to_all | solution.py:424
  8.7 1.1 %shift-left_add_fusion = s32[50000]{0:T(1024)S(1)} fusion(s32[50000]{0:T(1024)} %param.14, f32[50000]{0:T(1024)} %param.13), kind=kLoop, calls=%fused_computation.1 | loop fusion | flops 350000 | bytes 600000 | tf_op jit(solution)/shard_map/add | solution.py:271
  9.8 19.0 %forcing.1.force_ref = bf16[512,64]{1,0:T(8,128)(2,1)S(1)} custom-call(s32[512,128]{1,0:T(8,128)} %st_any.1, s32[512,128]{1,0:T(8,128)} %gi_any.1, s32[4,128]{1,0:T(4,128)} %bitcast.17, bf16[512,128]{1,0:T(8,128)(2,1)} %pr_any.1, bf16[64,3072]{1,0:T(8,128)(2,1)} %bitcast.16, s32[400,128]{1,0:T(8,128)S(1)} %pad_bitcast_fusion.word_ref), custom_call_target="tpu_custom_call" | custom-call | flops 20000000000 | bytes 2000000 | tf_op jit(solution)/shard_map/forcing/pallas_call | solution.py:281
  28.9 0.0 all-to-all-done.map_ref
  28.9 3.0 %collective-permute-start = (bf16[512,64]{1,0:T(8,128)(2,1)S(1)}, bf16[512,64]{1,0:T(8,128)(2,1)S(1)}, u32[]{:S(2)}, u32[]{:S(2)}) collective-permute-start(bf16[512,64]{1,0:T(8,128)(2,1)S(1)} %forcing.1.force_ref), channel_id=1, source_target_pairs={{0,1},{1,2},{2,3},{3,4},{4,5},{5,6},{6,7},{7,8},{8,9},{9,10},{10,1... | collective-permute-start | bytes 196616 | tf_op jit(solution)/shard_map/ppermute | solution.py:417
  31.9 3.1 %impulse_weights.1.wts = bf16[8192,256]{1,0:T(8,128)(2,1)S(1)} custom-call(bf16[4096,512]{1,0:T(8,128)(2,1)} %bitcast.15), custom_call_target="tpu_custom_call" | custom-call | flops 3000000000 | bytes 8000000 | tf_op jit(solution)/shard_map/impulse_weights/pallas_call | solution.py:330
  35.0 0.0 collective-permute-done.early_ref
  35.0 5.8 %local_stress.1 = bf16[128,512]{1,0:T(8,128)(2,1)S(1)} custom-call(bf16[512,64]{1,0:T(8,128)(2,1)S(1)} %collective-permute-done.early_ref, bf16[512,64]{1,0:T(8,128)(2,1)S(1)} %forcing.1.force_ref, bf16[16,8,128]{2,1,0:T(8,128)(2,1)S(1)} %all-to-all-done.map_ref, bf16[8192,256]{1,0:T(8,128)(2,1)S(1)} %impulse_weights.1.wts), custom_call_target="tpu_custom_call" | custom-call | flops 4000000000 | bytes 5000000 | tf_op jit(solution)/shard_map/local_stress/pallas_call | solution.py:402
  40.8 14.4 %all_to_all.24 = bf16[16,8,512]{2,1,0:T(8,128)(2,1)S(1)} all-to-all(bf16[16,8,512]{2,1,0:T(8,128)(2,1)S(1)} %bitcast.12), channel_id=1, replica_groups=mesh['sea'=2,'tm'=16] {'tm'}, dimensions={0} | all-to-all | bytes 262144 | tf_op jit(solution)/shard_map/all_to_all | solution.py:430
  55.2 0.7 %copy.11 = bf16[8,8192]{1,0:T(8,128)(2,1)} copy(bf16[8,8192]{1,0:T(8,128)(2,1)S(1)} %bitcast.13) | data formatting | bytes 262144
  (1 shorter events, 0.0 us)
Async XLA Ops:
  1.3 27.6 %all-to-all-start = ((bf16[16,8,128]{2,1,0:T(8,128)(2,1)}), bf16[16,8,128]{2,1,0:T(8,128)(2,1)S(1)}, u32[]{:S(2)}, u32[]{:S(2)}) async-start(bf16[16,8,128]{2,1,0:T(8,128)(2,1)} %broadcast_in_dim.2), calls=%async_computation | async-start | bytes 65536 | tf_op jit(solution)/shard_map/all_to_all | solution.py:424
  28.9 6.1 %collective-permute-start = (bf16[512,64]{1,0:T(8,128)(2,1)S(1)}, bf16[512,64]{1,0:T(8,128)(2,1)S(1)}, u32[]{:S(2)}, u32[]{:S(2)}) collective-permute-start(bf16[512,64]{1,0:T(8,128)(2,1)S(1)} %forcing.1.force_ref), channel_id=1, source_target_pairs={{0,1},{1,2},{2,3},{3,4},{4,5},{5,6},{6,7},{7,8},{8,9},{9,10},{10,1... | collective-permute-start | bytes 196616 | tf_op jit(solution)/shard_map/ppermute | solution.py:417
